TPU v7x, 32 devices: a whole 2x2x4 slice. The times are simulated.
32 devices in a mesh: blk: 8 (over y, x, core), dp: 4 (over z).
Axes of the slice: x: 2, y: 2, z: 4, core: 2. Of those that a mesh axis runs over, the one named last changes fastest.
Arguments:
- inputs: bfloat16 [1024, 2560], P('blk'), may hold values from -400 to 400
- gain: float32 [2560], replicated, may hold values from 0.1 to 1.9
- w_gate: bfloat16 [2560, 6912], P('blk', 'dp'), may hold values from -0.125 to 0.125
- w_up: bfloat16 [2560, 6912], P('blk', 'dp'), may hold values from -0.125 to 0.125
- upstream: bfloat16 [1024, 6912], P('blk', 'dp'), may hold values from -6 to 6
Outputs:
- hidden: bfloat16 [1024, 6912], P('blk', 'dp')
- grad_gate: float32 [2560, 6912], P('blk', 'dp')
- grad_up: float32 [2560, 6912], P('blk', 'dp')
- grad_input: bfloat16 [1024, 2560], P('blk', 'dp')
- grad_gain: float32 [2560], P('dp')
All inputs are finite; a program needn't handle non-finite values.
Results may differ from a plain program's by a relative error of at most 0.028.
Values may be sent and summed in bfloat16 or wider, within the bound.
A program may use at most 64 MiB of HBM per device.

v0:
```python
import jax
import jax.numpy as jnp
from jax import lax
from jax.sharding import PartitionSpec as P


def passed_along(value, axis, steps):
    count = lax.axis_size(axis)
    pairs = [(source, (source + steps) % count) for source in range(count)]
    return lax.ppermute(value, axis, pairs)


def column_terms(normed, block, block_rows, grad_gating, grad_upper):
    columns = lax.dynamic_slice_in_dim(normed, block * block_rows, block_rows, 1)
    dims = (((0,), (0,)), ((), ()))
    first = lax.dot_general(columns, grad_gating, dims, preferred_element_type=jnp.float32)
    second = lax.dot_general(columns, grad_upper, dims, preferred_element_type=jnp.float32)
    return (first, second)


def per_device(inputs, gain, w_gate, w_up, upstream):
    wide_input = inputs.astype(jnp.float32)
    root_mean = jnp.sqrt(jnp.mean(wide_input * wide_input, axis=1, keepdims=True) + 1e-05)
    unit_input = wide_input / root_mean
    normed = (unit_input * gain).astype(jnp.bfloat16)
    gate_whole, up_whole = (
        lax.all_gather(w_gate, "blk", axis=0, tiled=True),
        lax.all_gather(w_up, "blk", axis=0, tiled=True),
    )
    gate_pre = jnp.dot(normed, gate_whole, preferred_element_type=jnp.float32)
    up_pre = jnp.dot(normed, up_whole, preferred_element_type=jnp.float32)
    sigmoid_gate = jax.nn.sigmoid(gate_pre)
    activated = gate_pre * sigmoid_gate
    hidden = (activated * up_pre).astype(jnp.bfloat16)
    upstream_wide = upstream.astype(jnp.float32)
    grad_upper = (upstream_wide * activated).astype(jnp.bfloat16)
    grad_gating = (
        upstream_wide * up_pre * sigmoid_gate * (1.0 + gate_pre * (1.0 - sigmoid_gate))
    ).astype(jnp.bfloat16)
    local_part = jnp.dot(grad_gating, gate_whole.T, preferred_element_type=jnp.float32) + jnp.dot(
        grad_upper, up_whole.T, preferred_element_type=jnp.float32
    )
    back_normed = lax.optimization_barrier(local_part.astype(jnp.bfloat16)).astype(jnp.float32)
    cycle_size = lax.axis_size("blk")
    block_rows = w_gate.shape[0]
    position = lax.axis_index("blk")

    def advance(index, totals):
        totals = (
            passed_along(totals[0].astype(jnp.bfloat16), "blk", 1).astype(jnp.float32),
            passed_along(totals[1].astype(jnp.bfloat16), "blk", 1).astype(jnp.float32),
        )
        fresh = column_terms(
            normed, (position - index - 1) % cycle_size, block_rows, grad_gating, grad_upper
        )
        return (totals[0] + fresh[0], totals[1] + fresh[1])

    start = column_terms(normed, (position - 1) % cycle_size, block_rows, grad_gating, grad_upper)
    grad_gate, grad_up = lax.fori_loop(1, cycle_size, advance, start)
    feature_count = back_normed.shape[1] // lax.axis_size("dp")
    feature_start = lax.axis_index("dp") * feature_count
    gain_slice = lax.dynamic_slice_in_dim(gain, feature_start, feature_count, 0)
    unit_slice = lax.dynamic_slice_in_dim(unit_input, feature_start, feature_count, 1)
    own_sums = lax.psum_scatter(
        back_normed.astype(jnp.bfloat16), "dp", scatter_dimension=1, tiled=True
    ).astype(jnp.float32)
    token_totals = lax.psum(jnp.sum(own_sums * gain_slice * unit_slice, axis=1), "dp")
    token_means = token_totals[:, None] / back_normed.shape[1]
    grad_input = ((own_sums * gain_slice - unit_slice * token_means) / root_mean).astype(
        jnp.bfloat16
    )
    grad_gain = lax.psum(jnp.sum(own_sums * unit_slice, axis=0), "blk")
    return (hidden, grad_gate, grad_up, grad_input, grad_gain)


def solution(mesh):
    return jax.shard_map(
        per_device,
        mesh=mesh,
        in_specs=(P("blk", None), P(), P("blk", "dp"), P("blk", "dp"), P("blk", "dp")),
        out_specs=(P("blk", "dp"), P("blk", "dp"), P("blk", "dp"), P("blk", "dp"), P("dp")),
        check_vma=False,
    )
```

profile of v0, /device:TPU:0, one launch (start us, length us, event | category | flops | bytes accessed | tf_op | source)
XLA Modules:
  0.0 433.8 jit_solution(14282839376861347590)
XLA Ops:
  9.0 1.3 convert_divide_fusion
  10.3 60.1 %all-gather.3.cloned.1.call-done = bf16[2560,1728]{1,0:T(8,128)(2,1)} async-done(((bf16[320,1728]{1,0:T(8,128)(2,1)}), bf16[2560,1728]{1,0:T(8,128)(2,1)}) %all-gather.3.cloned.1.call-update) | async-done | bytes 8847376 | tf_op jit(solution)/shard_map/all_gather | solution.py:27
  70.4 7.3 %fusion.29 = f32[128,1728]{0,1:T(8,128)S(1)} fusion(bf16[128,2560]{1,0:T(8,128)(2,1)S(1)} %get-tuple-element.268, bf16[2560,1728]{1,0:T(8,128)(2,1)} %all-gather.3.cloned.1.call-done), kind=kOutput, calls=%fused_computation.39 | convolution fusion | flops 1132462080 | bytes 10387456 | tf_op jit(solution)/shard_map/dot_general | solution.py:30
  77.7 52.3 %all-gather.5.cloned.1.call-done = bf16[2560,1728]{1,0:T(8,128)(2,1)} async-done(((bf16[320,1728]{1,0:T(8,128)(2,1)}), bf16[2560,1728]{1,0:T(8,128)(2,1)}) %all-gather.5.cloned.1.call-update) | async-done | bytes 8847376 | tf_op jit(solution)/shard_map/all_gather | solution.py:28
  130.0 8.3 %fusion.14 = (bf16[128,1728]{0,1:T(8,128)(2,1)S(1)}, bf16[128,1728]{0,1:T(8,128)(2,1)}, bf16[128,1728]{0,1:T(8,128)(2,1)S(1)}) fusion(bf16[128,1728]{0,1:T(8,128)(2,1)S(1)} %copy-done.11, f32[128,1728]{0,1:T(8,128)S(1)} %fusion.29, bf16[128,2560]{1,0:T(8,128)(2,1)S(1)} %get-tuple-element.268, bf16[2560,1728]{1,0:T(8,128)(2,1)} %all-gather.5.cloned.1.call-done), kind=kOutput, calls=%fused_computation.18 | convolution fusion | flops 1136001024 | bytes 12156928 | tf_op jit(solution)/shard_map/dot_general | solution.py:31
  138.3 3.2 fusion.30
  142.1 3.2 fusion.10
  145.2 1.1 copy.14
  146.5 1.0 copy.12
  147.5 1.2 copy.13
  149.7 2.0 fusion.25
  151.6 17.0 %reduce-scatter.4.cloned.1.call-done = bf16[640,128]{1,0:T(8,128)(2,1)} async-done(((bf16[2560,128]{1,0:T(8,128)(2,1)}), bf16[640,128]{1,0:T(8,128)(2,1)}) %reduce-scatter.4.cloned.1.call-update) | async-done | bytes 163856
  168.7 1.1 copy.15
  169.7 1.1 fusion.22
  170.8 9.7 %psum.14 = f32[128]{0:T(128)S(1)} all-reduce(f32[128]{0:T(128)S(1)} %get-tuple-element.201), channel_id=1, replica_groups=mesh['blk'=8,'dp'=4] {'dp'}, use_global_device_ids=true, to_apply=%region_5.6 | all-reduce | flops 128 | bytes 1024 | tf_op jit(solution)/shard_map/psum | solution.py:67
  180.5 1.8 fusion.21
  182.3 12.4 %psum.15 = f32[640]{0:T(1024)} all-reduce(f32[640]{0:T(1024)S(1)} %get-tuple-element.200), channel_id=1, replica_groups=mesh['blk'=8,'dp'=4] {'blk'}, use_global_device_ids=true, to_apply=%region_7.8 | all-reduce | flops 640 | bytes 5120 | tf_op jit(solution)/shard_map/psum | solution.py:72
  194.7 231.2 %while.17 = (s32[]{:T(128)}, f32[320,1728]{1,0:T(8,128)}, f32[320,1728]{1,0:T(8,128)S(1)}, s32[]{:T(128)}, bf16[128,2560]{1,0:T(8,128)(2,1)S(1)}, /*index=5*/bf1...) while((s32[]{:T(128)}, f32[320,1728]{1,0:T(8,128)}, ...), condition=%wide.region_2.3_spmd, body=%wide.region_1.2_spmd.sunk | while | flops 286433280 | bytes 41828856 | solution.py:59
  195.7 1.5 copy-done.1
  197.2 1.1 convert_element_type.122
  198.3 13.6 %collective-permute-done.1 = bf16[320,1728]{1,0:T(8,128)(2,1)S(1)} collective-permute-done((bf16[320,1728]{1,0:T(8,128)(2,1)S(1)}, bf16[320,1728]{1,0:T(8,128)(2,1)S(1)}, u32[]{:S(2)}, u32[]{:S(2)}) %collective-permute-start.1) | collective-permute-done | bytes 1105952 | tf_op jit(solution)/shard_map/while/body/eval_jaxpr/ppermute | solution.py:10
  211.9 1.0 copy-done.3
  212.9 2.0 convert_add_fusion.5
  214.9 9.3 %collective-permute-done = bf16[320,1728]{1,0:T(8,128)(2,1)} collective-permute-done((bf16[320,1728]{1,0:T(8,128)(2,1)}, bf16[320,1728]{1,0:T(8,128)(2,1)}, u32[]{:S(2)}, u32[]{:S(2)}) %collective-permute-start) | collective-permute-done | bytes 1105952 | tf_op jit(solution)/shard_map/while/body/eval_jaxpr/ppermute | solution.py:10
  224.3 3.4 convert_add_fusion.4
  228.8 1.5 copy-done.1
  230.2 1.1 convert_element_type.122
  231.3 13.6 %collective-permute-done.1 = bf16[320,1728]{1,0:T(8,128)(2,1)S(1)} collective-permute-done((bf16[320,1728]{1,0:T(8,128)(2,1)S(1)}, bf16[320,1728]{1,0:T(8,128)(2,1)S(1)}, u32[]{:S(2)}, u32[]{:S(2)}) %collective-permute-start.1) | collective-permute-done | bytes 1105952 | tf_op jit(solution)/shard_map/while/body/eval_jaxpr/ppermute | solution.py:10
  244.9 1.0 copy-done.3
  245.9 2.0 convert_add_fusion.5
  248.0 9.3 %collective-permute-done = bf16[320,1728]{1,0:T(8,128)(2,1)} collective-permute-done((bf16[320,1728]{1,0:T(8,128)(2,1)}, bf16[320,1728]{1,0:T(8,128)(2,1)}, u32[]{:S(2)}, u32[]{:S(2)}) %collective-permute-start) | collective-permute-done | bytes 1105952 | tf_op jit(solution)/shard_map/while/body/eval_jaxpr/ppermute | solution.py:10
  257.3 3.4 convert_add_fusion.4
  261.8 1.5 copy-done.1
  263.3 1.1 convert_element_type.122
  264.4 13.6 %collective-permute-done.1 = bf16[320,1728]{1,0:T(8,128)(2,1)S(1)} collective-permute-done((bf16[320,1728]{1,0:T(8,128)(2,1)S(1)}, bf16[320,1728]{1,0:T(8,128)(2,1)S(1)}, u32[]{:S(2)}, u32[]{:S(2)}) %collective-permute-start.1) | collective-permute-done | bytes 1105952 | tf_op jit(solution)/shard_map/while/body/eval_jaxpr/ppermute | solution.py:10
  278.0 1.0 copy-done.3
  279.0 2.0 convert_add_fusion.5
  281.0 9.3 %collective-permute-done = bf16[320,1728]{1,0:T(8,128)(2,1)} collective-permute-done((bf16[320,1728]{1,0:T(8,128)(2,1)}, bf16[320,1728]{1,0:T(8,128)(2,1)}, u32[]{:S(2)}, u32[]{:S(2)}) %collective-permute-start) | collective-permute-done | bytes 1105952 | tf_op jit(solution)/shard_map/while/body/eval_jaxpr/ppermute | solution.py:10
  290.3 3.4 convert_add_fusion.4
  294.8 1.5 copy-done.1
  296.3 1.1 convert_element_type.122
  297.4 13.6 %collective-permute-done.1 = bf16[320,1728]{1,0:T(8,128)(2,1)S(1)} collective-permute-done((bf16[320,1728]{1,0:T(8,128)(2,1)S(1)}, bf16[320,1728]{1,0:T(8,128)(2,1)S(1)}, u32[]{:S(2)}, u32[]{:S(2)}) %collective-permute-start.1) | collective-permute-done | bytes 1105952 | tf_op jit(solution)/shard_map/while/body/eval_jaxpr/ppermute | solution.py:10
  312.0 2.0 convert_add_fusion.5
  314.0 9.3 %collective-permute-done = bf16[320,1728]{1,0:T(8,128)(2,1)} collective-permute-done((bf16[320,1728]{1,0:T(8,128)(2,1)}, bf16[320,1728]{1,0:T(8,128)(2,1)}, u32[]{:S(2)}, u32[]{:S(2)}) %collective-permute-start) | collective-permute-done | bytes 1105952 | tf_op jit(solution)/shard_map/while/body/eval_jaxpr/ppermute | solution.py:10
  323.4 3.4 convert_add_fusion.4
  327.8 1.5 copy-done.1
  329.3 1.1 convert_element_type.122
  330.4 13.6 %collective-permute-done.1 = bf16[320,1728]{1,0:T(8,128)(2,1)S(1)} collective-permute-done((bf16[320,1728]{1,0:T(8,128)(2,1)S(1)}, bf16[320,1728]{1,0:T(8,128)(2,1)S(1)}, u32[]{:S(2)}, u32[]{:S(2)}) %collective-permute-start.1) | collective-permute-done | bytes 1105952 | tf_op jit(solution)/shard_map/while/body/eval_jaxpr/ppermute | solution.py:10
  345.0 2.0 convert_add_fusion.5
  347.1 9.3 %collective-permute-done = bf16[320,1728]{1,0:T(8,128)(2,1)} collective-permute-done((bf16[320,1728]{1,0:T(8,128)(2,1)}, bf16[320,1728]{1,0:T(8,128)(2,1)}, u32[]{:S(2)}, u32[]{:S(2)}) %collective-permute-start) | collective-permute-done | bytes 1105952 | tf_op jit(solution)/shard_map/while/body/eval_jaxpr/ppermute | solution.py:10
  356.4 3.4 convert_add_fusion.4
  360.9 1.5 copy-done.1
  362.3 1.1 convert_element_type.122
  363.5 13.6 %collective-permute-done.1 = bf16[320,1728]{1,0:T(8,128)(2,1)S(1)} collective-permute-done((bf16[320,1728]{1,0:T(8,128)(2,1)S(1)}, bf16[320,1728]{1,0:T(8,128)(2,1)S(1)}, u32[]{:S(2)}, u32[]{:S(2)}) %collective-permute-start.1) | collective-permute-done | bytes 1105952 | tf_op jit(solution)/shard_map/while/body/eval_jaxpr/ppermute | solution.py:10
  378.0 2.0 convert_add_fusion.5
  380.1 9.3 %collective-permute-done = bf16[320,1728]{1,0:T(8,128)(2,1)} collective-permute-done((bf16[320,1728]{1,0:T(8,128)(2,1)}, bf16[320,1728]{1,0:T(8,128)(2,1)}, u32[]{:S(2)}, u32[]{:S(2)}) %collective-permute-start) | collective-permute-done | bytes 1105952 | tf_op jit(solution)/shard_map/while/body/eval_jaxpr/ppermute | solution.py:10
  389.4 3.4 convert_add_fusion.4
  393.9 1.5 copy-done.1
  395.4 1.1 convert_element_type.122
  396.5 13.6 %collective-permute-done.1 = bf16[320,1728]{1,0:T(8,128)(2,1)S(1)} collective-permute-done((bf16[320,1728]{1,0:T(8,128)(2,1)S(1)}, bf16[320,1728]{1,0:T(8,128)(2,1)S(1)}, u32[]{:S(2)}, u32[]{:S(2)}) %collective-permute-start.1) | collective-permute-done | bytes 1105952 | tf_op jit(solution)/shard_map/while/body/eval_jaxpr/ppermute | solution.py:10
  411.1 2.0 convert_add_fusion.5
  413.1 9.3 %collective-permute-done = bf16[320,1728]{1,0:T(8,128)(2,1)} collective-permute-done((bf16[320,1728]{1,0:T(8,128)(2,1)}, bf16[320,1728]{1,0:T(8,128)(2,1)}, u32[]{:S(2)}, u32[]{:S(2)}) %collective-permute-start) | collective-permute-done | bytes 1105952 | tf_op jit(solution)/shard_map/while/body/eval_jaxpr/ppermute | solution.py:10
  422.5 3.4 convert_add_fusion.4
  425.9 1.4 copy-done
  (93 shorter events, 14.8 us)
Async XLA Ops:
  7.2 1.6 copy-start.9
  7.2 1.8 copy-start.10
  7.2 63.2 %all-gather.3.cloned.1.call-start = ((), (), s32[]{:S(2)}) async-start(), calls=%async_computation.1 | async-start | bytes 10321920 | tf_op jit(solution)/shard_map/all_gather | solution.py:27
  7.9 122.1 %all-gather.5.cloned.1.call-start = ((), (), s32[]{:S(2)}) async-start(), calls=%async_computation.2 | async-start | bytes 10321920 | tf_op jit(solution)/shard_map/all_gather | solution.py:28
  8.7 160.0 %reduce-scatter.4.cloned.1.call-start = ((), (), s32[]{:S(2)}) async-start(), calls=%async_computation.3 | async-start | bytes 819200
  70.4 59.6 %copy-start.11 = (bf16[128,1728]{0,1:T(8,128)(2,1)S(1)}, bf16[128,1728]{0,1:T(8,128)(2,1)}, u32[]{:S(2)}) copy-start(bf16[128,1728]{0,1:T(8,128)(2,1)} %param.11) | copy-start | bytes 1327108
  130.0 8.3 %copy-start.2 = (bf16[2560,1728]{1,0:T(8,128)(2,1)S(1)}, bf16[2560,1728]{1,0:T(8,128)(2,1)}, u32[]{:S(2)}) copy-start(bf16[2560,1728]{1,0:T(8,128)(2,1)} %all-gather.3.cloned.1.call-done) | copy-start | bytes 26542084
  138.3 8.2 %copy-start.7 = (bf16[128,1728]{0,1:T(8,128)(2,1)}, bf16[128,1728]{0,1:T(8,128)(2,1)S(1)}, u32[]{:S(2)}) copy-start(bf16[128,1728]{0,1:T(8,128)(2,1)S(1)} %get-tuple-element.216) | copy-start | bytes 1327108
  138.3 3.8 copy-start.6
  148.7 1.0 copy-start.8
  194.7 0.9 copy-start.4
  195.5 1.6 copy-start.1
  195.7 16.2 %collective-permute-start.1 = (bf16[320,1728]{1,0:T(8,128)(2,1)S(1)}, bf16[320,1728]{1,0:T(8,128)(2,1)S(1)}, u32[]{:S(2)}, u32[]{:S(2)}) collective-permute-start(bf16[320,1728]{1,0:T(8,128)(2,1)S(1)} %convert_element_type.123), channel_id=1, source_target_pairs={{0,4},{4,8},{8,12},{12,16},{16,20},{20,24},{24,28},{28,0},{1,5},{5... | collective-permute-start | bytes 3317768 | tf_op jit(solution)/shard_map/while/body/eval_jaxpr/ppermute | solution.py:10
  198.3 26.0 %collective-permute-start = (bf16[320,1728]{1,0:T(8,128)(2,1)}, bf16[320,1728]{1,0:T(8,128)(2,1)}, u32[]{:S(2)}, u32[]{:S(2)}) collective-permute-start(bf16[320,1728]{1,0:T(8,128)(2,1)} %convert_element_type.122), channel_id=1, source_target_pairs={{0,4},{4,8},{8,12},{12,16},{16,20},{20,24},{24,28},{28,0},{1,5},{5... | collective-permute-start | bytes 3317768 | tf_op jit(solution)/shard_map/while/body/eval_jaxpr/ppermute | solution.py:10
  211.9 1.0 copy-start.3
  214.9 12.8 %copy-start.5 = (bf16[128,2560]{1,0:T(8,128)(2,1)S(1)}, bf16[128,2560]{1,0:T(8,128)(2,1)}, u32[]{:S(2)}) copy-start(bf16[128,2560]{1,0:T(8,128)(2,1)} %copy-done.4) | copy-start | bytes 1966084 | tf_op jit(solution)/shard_map/while
  227.7 0.9 copy-start.4
  228.6 1.6 copy-start.1
  228.7 16.2 %collective-permute-start.1 = (bf16[320,1728]{1,0:T(8,128)(2,1)S(1)}, bf16[320,1728]{1,0:T(8,128)(2,1)S(1)}, u32[]{:S(2)}, u32[]{:S(2)}) collective-permute-start(bf16[320,1728]{1,0:T(8,128)(2,1)S(1)} %convert_element_type.123), channel_id=1, source_target_pairs={{0,4},{4,8},{8,12},{12,16},{16,20},{20,24},{24,28},{28,0},{1,5},{5... | collective-permute-start | bytes 3317768 | tf_op jit(solution)/shard_map/while/body/eval_jaxpr/ppermute | solution.py:10
  231.3 26.0 %collective-permute-start = (bf16[320,1728]{1,0:T(8,128)(2,1)}, bf16[320,1728]{1,0:T(8,128)(2,1)}, u32[]{:S(2)}, u32[]{:S(2)}) collective-permute-start(bf16[320,1728]{1,0:T(8,128)(2,1)} %convert_element_type.122), channel_id=1, source_target_pairs={{0,4},{4,8},{8,12},{12,16},{16,20},{20,24},{24,28},{28,0},{1,5},{5... | collective-permute-start | bytes 3317768 | tf_op jit(solution)/shard_map/while/body/eval_jaxpr/ppermute | solution.py:10
  244.9 1.0 copy-start.3
  248.0 12.8 %copy-start.5 = (bf16[128,2560]{1,0:T(8,128)(2,1)S(1)}, bf16[128,2560]{1,0:T(8,128)(2,1)}, u32[]{:S(2)}) copy-start(bf16[128,2560]{1,0:T(8,128)(2,1)} %copy-done.4) | copy-start | bytes 1966084 | tf_op jit(solution)/shard_map/while
  260.7 0.9 copy-start.4
  261.6 1.6 copy-start.1
  261.7 16.2 %collective-permute-start.1 = (bf16[320,1728]{1,0:T(8,128)(2,1)S(1)}, bf16[320,1728]{1,0:T(8,128)(2,1)S(1)}, u32[]{:S(2)}, u32[]{:S(2)}) collective-permute-start(bf16[320,1728]{1,0:T(8,128)(2,1)S(1)} %convert_element_type.123), channel_id=1, source_target_pairs={{0,4},{4,8},{8,12},{12,16},{16,20},{20,24},{24,28},{28,0},{1,5},{5... | collective-permute-start | bytes 3317768 | tf_op jit(solution)/shard_map/while/body/eval_jaxpr/ppermute | solution.py:10
  264.4 26.0 %collective-permute-start = (bf16[320,1728]{1,0:T(8,128)(2,1)}, bf16[320,1728]{1,0:T(8,128)(2,1)}, u32[]{:S(2)}, u32[]{:S(2)}) collective-permute-start(bf16[320,1728]{1,0:T(8,128)(2,1)} %convert_element_type.122), channel_id=1, source_target_pairs={{0,4},{4,8},{8,12},{12,16},{16,20},{20,24},{24,28},{28,0},{1,5},{5... | collective-permute-start | bytes 3317768 | tf_op jit(solution)/shard_map/while/body/eval_jaxpr/ppermute | solution.py:10
  278.0 1.0 copy-start.3
  281.0 12.8 %copy-start.5 = (bf16[128,2560]{1,0:T(8,128)(2,1)S(1)}, bf16[128,2560]{1,0:T(8,128)(2,1)}, u32[]{:S(2)}) copy-start(bf16[128,2560]{1,0:T(8,128)(2,1)} %copy-done.4) | copy-start | bytes 1966084 | tf_op jit(solution)/shard_map/while
  293.8 0.9 copy-start.4
  294.6 1.6 copy-start.1
  294.8 16.2 %collective-permute-start.1 = (bf16[320,1728]{1,0:T(8,128)(2,1)S(1)}, bf16[320,1728]{1,0:T(8,128)(2,1)S(1)}, u32[]{:S(2)}, u32[]{:S(2)}) collective-permute-start(bf16[320,1728]{1,0:T(8,128)(2,1)S(1)} %convert_element_type.123), channel_id=1, source_target_pairs={{0,4},{4,8},{8,12},{12,16},{16,20},{20,24},{24,28},{28,0},{1,5},{5... | collective-permute-start | bytes 3317768 | tf_op jit(solution)/shard_map/while/body/eval_jaxpr/ppermute | solution.py:10
  297.4 26.0 %collective-permute-start = (bf16[320,1728]{1,0:T(8,128)(2,1)}, bf16[320,1728]{1,0:T(8,128)(2,1)}, u32[]{:S(2)}, u32[]{:S(2)}) collective-permute-start(bf16[320,1728]{1,0:T(8,128)(2,1)} %convert_element_type.122), channel_id=1, source_target_pairs={{0,4},{4,8},{8,12},{12,16},{16,20},{20,24},{24,28},{28,0},{1,5},{5... | collective-permute-start | bytes 3317768 | tf_op jit(solution)/shard_map/while/body/eval_jaxpr/ppermute | solution.py:10
  311.0 1.0 copy-start.3
  314.0 12.8 %copy-start.5 = (bf16[128,2560]{1,0:T(8,128)(2,1)S(1)}, bf16[128,2560]{1,0:T(8,128)(2,1)}, u32[]{:S(2)}) copy-start(bf16[128,2560]{1,0:T(8,128)(2,1)} %copy-done.4) | copy-start | bytes 1966084 | tf_op jit(solution)/shard_map/while
  326.8 0.9 copy-start.4
  327.7 1.6 copy-start.1
  327.8 16.2 %collective-permute-start.1 = (bf16[320,1728]{1,0:T(8,128)(2,1)S(1)}, bf16[320,1728]{1,0:T(8,128)(2,1)S(1)}, u32[]{:S(2)}, u32[]{:S(2)}) collective-permute-start(bf16[320,1728]{1,0:T(8,128)(2,1)S(1)} %convert_element_type.123), channel_id=1, source_target_pairs={{0,4},{4,8},{8,12},{12,16},{16,20},{20,24},{24,28},{28,0},{1,5},{5... | collective-permute-start | bytes 3317768 | tf_op jit(solution)/shard_map/while/body/eval_jaxpr/ppermute | solution.py:10
  330.4 26.0 %collective-permute-start = (bf16[320,1728]{1,0:T(8,128)(2,1)}, bf16[320,1728]{1,0:T(8,128)(2,1)}, u32[]{:S(2)}, u32[]{:S(2)}) collective-permute-start(bf16[320,1728]{1,0:T(8,128)(2,1)} %convert_element_type.122), channel_id=1, source_target_pairs={{0,4},{4,8},{8,12},{12,16},{16,20},{20,24},{24,28},{28,0},{1,5},{5... | collective-permute-start | bytes 3317768 | tf_op jit(solution)/shard_map/while/body/eval_jaxpr/ppermute | solution.py:10
  344.0 1.0 copy-start.3
  347.0 12.8 %copy-start.5 = (bf16[128,2560]{1,0:T(8,128)(2,1)S(1)}, bf16[128,2560]{1,0:T(8,128)(2,1)}, u32[]{:S(2)}) copy-start(bf16[128,2560]{1,0:T(8,128)(2,1)} %copy-done.4) | copy-start | bytes 1966084 | tf_op jit(solution)/shard_map/while
  359.8 0.9 copy-start.4
  360.7 1.6 copy-start.1
  360.8 16.2 %collective-permute-start.1 = (bf16[320,1728]{1,0:T(8,128)(2,1)S(1)}, bf16[320,1728]{1,0:T(8,128)(2,1)S(1)}, u32[]{:S(2)}, u32[]{:S(2)}) collective-permute-start(bf16[320,1728]{1,0:T(8,128)(2,1)S(1)} %convert_element_type.123), channel_id=1, source_target_pairs={{0,4},{4,8},{8,12},{12,16},{16,20},{20,24},{24,28},{28,0},{1,5},{5... | collective-permute-start | bytes 3317768 | tf_op jit(solution)/shard_map/while/body/eval_jaxpr/ppermute | solution.py:10
  363.4 26.0 %collective-permute-start = (bf16[320,1728]{1,0:T(8,128)(2,1)}, bf16[320,1728]{1,0:T(8,128)(2,1)}, u32[]{:S(2)}, u32[]{:S(2)}) collective-permute-start(bf16[320,1728]{1,0:T(8,128)(2,1)} %convert_element_type.122), channel_id=1, source_target_pairs={{0,4},{4,8},{8,12},{12,16},{16,20},{20,24},{24,28},{28,0},{1,5},{5... | collective-permute-start | bytes 3317768 | tf_op jit(solution)/shard_map/while/body/eval_jaxpr/ppermute | solution.py:10
  377.0 1.0 copy-start.3
  380.1 12.8 %copy-start.5 = (bf16[128,2560]{1,0:T(8,128)(2,1)S(1)}, bf16[128,2560]{1,0:T(8,128)(2,1)}, u32[]{:S(2)}) copy-start(bf16[128,2560]{1,0:T(8,128)(2,1)} %copy-done.4) | copy-start | bytes 1966084 | tf_op jit(solution)/shard_map/while
  392.8 0.9 copy-start.4
  393.7 1.6 copy-start.1
  393.8 16.2 %collective-permute-start.1 = (bf16[320,1728]{1,0:T(8,128)(2,1)S(1)}, bf16[320,1728]{1,0:T(8,128)(2,1)S(1)}, u32[]{:S(2)}, u32[]{:S(2)}) collective-permute-start(bf16[320,1728]{1,0:T(8,128)(2,1)S(1)} %convert_element_type.123), channel_id=1, source_target_pairs={{0,4},{4,8},{8,12},{12,16},{16,20},{20,24},{24,28},{28,0},{1,5},{5... | collective-permute-start | bytes 3317768 | tf_op jit(solution)/shard_map/while/body/eval_jaxpr/ppermute | solution.py:10
  396.5 26.0 %collective-permute-start = (bf16[320,1728]{1,0:T(8,128)(2,1)}, bf16[320,1728]{1,0:T(8,128)(2,1)}, u32[]{:S(2)}, u32[]{:S(2)}) collective-permute-start(bf16[320,1728]{1,0:T(8,128)(2,1)} %convert_element_type.122), channel_id=1, source_target_pairs={{0,4},{4,8},{8,12},{12,16},{16,20},{20,24},{24,28},{28,0},{1,5},{5... | collective-permute-start | bytes 3317768 | tf_op jit(solution)/shard_map/while/body/eval_jaxpr/ppermute | solution.py:10
  410.1 1.0 copy-start.3
  413.1 12.8 %copy-start.5 = (bf16[128,2560]{1,0:T(8,128)(2,1)S(1)}, bf16[128,2560]{1,0:T(8,128)(2,1)}, u32[]{:S(2)}) copy-start(bf16[128,2560]{1,0:T(8,128)(2,1)} %copy-done.4) | copy-start | bytes 1966084 | tf_op jit(solution)/shard_map/while
  425.9 1.4 copy-start
Sparse Core Ops, SparseCore 0:
  9.9 60.4 all-gather.2
  72.2 57.7 all-gather.4
  146.5 22.1 reduce-scatter.3
where the time goes:
time: 435 us; the launch traced here: 434 us
  waiting for transfers between devices  291 us (67%)
  matrix products  62.5 us (14%)
  local copies, waits for them, and re-layouts  30.2 us (7%)
  blocking collectives  22.1 us (5%)
  between operations  13.8 us (3%)
  other arithmetic  13.1 us (3%)
    ppermute x14, waiting for transfers between devices, passed_along(): return lax.ppermute(value, axis, pairs)  160 us
    all_gather x1, waiting for transfers between devices, per_device(): lax.all_gather(w_gate, 'blk', axis=0, tiled=True)  60.1 us
    all_gather x1, waiting for transfers between devices, per_device(): lax.all_gather(w_up, 'blk', axis=0, tiled=True)  52.3 us
    dot_general x8, matrix products, column_terms(): lax.dot_general(columns, grad_gating, dims, preferred_element_type=jnp.fl...  25.9 us
    while x56, local copies, waits for them, and re-layouts  23.3 us
    unnamed x4, waiting for transfers between devices  18.4 us
    dot_general x8, matrix products, column_terms(): lax.dot_general(columns, grad_upper, dims, preferred_element_type=jnp.flo...  14.8 us
    psum x1, blocking collectives, per_device(): grad_gain = lax.psum(jnp.sum(own_sums * unit_slice, axis=0), 'blk')  12.4 us
  transfers between devices with their start and end apart: 17, of which 17 were waited for; matrix products, arithmetic and copies ran while one was open for 8% of the time, Pallas kernels for 0%

commit v1 on v0

v1 whole, which is shorter than its diff:
```python
import jax
import jax.numpy as jnp
from jax import lax
from jax.sharding import PartitionSpec as P


def per_device(inputs, gain, w_gate, w_up, upstream):
    wide_input = inputs.astype(jnp.float32)
    root_mean = jnp.sqrt(jnp.mean(wide_input * wide_input, axis=1, keepdims=True) + 1e-05)
    unit_input = wide_input / root_mean
    normed = (unit_input * gain).astype(jnp.bfloat16)
    columns = lax.all_to_all(normed, "blk", split_axis=1, concat_axis=0, tiled=True)
    gate_part = jnp.dot(columns, w_gate, preferred_element_type=jnp.float32).astype(jnp.bfloat16)
    up_part = jnp.dot(columns, w_up, preferred_element_type=jnp.float32).astype(jnp.bfloat16)
    gate_pre = lax.psum_scatter(gate_part, "blk", scatter_dimension=0, tiled=True).astype(jnp.float32)
    up_pre = lax.psum_scatter(up_part, "blk", scatter_dimension=0, tiled=True).astype(jnp.float32)
    sigmoid_gate = jax.nn.sigmoid(gate_pre)
    activated = gate_pre * sigmoid_gate
    hidden = (activated * up_pre).astype(jnp.bfloat16)
    upstream_wide = upstream.astype(jnp.float32)
    back_up = (upstream_wide * activated).astype(jnp.bfloat16)
    back_gate = (
        upstream_wide * up_pre * sigmoid_gate * (1.0 + gate_pre * (1.0 - sigmoid_gate))
    ).astype(jnp.bfloat16)
    all_up = lax.all_gather(back_up, "blk", axis=0, tiled=True)
    all_gate = lax.all_gather(back_gate, "blk", axis=0, tiled=True)
    over_tokens = (((0,), (0,)), ((), ()))
    over_hidden = (((1,), (1,)), ((), ()))
    grad_up = lax.dot_general(columns, all_up, over_tokens, preferred_element_type=jnp.float32)
    grad_gate = lax.dot_general(columns, all_gate, over_tokens, preferred_element_type=jnp.float32)
    part = lax.dot_general(
        all_gate, w_gate, over_hidden, preferred_element_type=jnp.float32
    ) + lax.dot_general(all_up, w_up, over_hidden, preferred_element_type=jnp.float32)
    part = lax.all_to_all(
        part.astype(jnp.bfloat16), "blk", split_axis=0, concat_axis=1, tiled=True
    )
    feature_count = inputs.shape[1] // lax.axis_size("dp")
    feature_start = lax.axis_index("dp") * feature_count
    gain_slice = lax.dynamic_slice_in_dim(gain, feature_start, feature_count, 0)
    unit_slice = lax.dynamic_slice_in_dim(unit_input, feature_start, feature_count, 1)
    own_sums = lax.psum_scatter(part, "dp", scatter_dimension=1, tiled=True).astype(jnp.float32)
    token_totals = lax.psum(jnp.sum(own_sums * gain_slice * unit_slice, axis=1), "dp")
    token_means = token_totals[:, None] / inputs.shape[1]
    grad_input = ((own_sums * gain_slice - unit_slice * token_means) / root_mean).astype(
        jnp.bfloat16
    )
    grad_gain = lax.psum(jnp.sum(own_sums * unit_slice, axis=0), "blk")
    return (hidden, grad_gate, grad_up, grad_input, grad_gain)


def solution(mesh):
    return jax.shard_map(
        per_device,
        mesh=mesh,
        in_specs=(P("blk", None), P(), P("blk", "dp"), P("blk", "dp"), P("blk", "dp")),
        out_specs=(P("blk", "dp"), P("blk", "dp"), P("blk", "dp"), P("blk", "dp"), P("dp")),
        check_vma=False,
    )
```

time: 435 us -> 283 us (0.65)
  waiting for transfers between devices: 291 us -> 168 us
  matrix products: 62.5 us -> 25.2 us
  blocking collectives: 22.1 us -> 52.6 us
  local copies, waits for them, and re-layouts: 30.2 us -> 16.9 us
  other arithmetic: 13.1 us -> 5.58 us
    ppermute x14 -> x0, waiting for transfers between devices: 160 us -> none  [passed_along(): return lax.ppermute(value, axis, pairs)]
    unnamed x4 -> x7, waiting for transfers between devices: 18.4 us -> 88.9 us
    all_gather x2, waiting for transfers between devices: 112 us -> 66 us  [the longest x1 34.1 us: per_device(): all_gate = lax.all_gather(back_gate, 'blk', axis=0, tiled=True)]
    dot_general x20 -> x6, matrix products: 62.5 us -> 25.2 us  [the longest x1 5.17 us: per_device(): jnp.dot(columns, w_up, preferred_element_type=jnp.float32)]
    all_to_all x0 -> x2, blocking collectives: none -> 30.5 us  [the longest x1 16.1 us: per_device(): lax.all_to_all(normed, 'blk', split_axis=1, concat_axis=0, tiled=True)]
    while x58 -> x0, local copies, waits for them, and re-layouts: 25.5 us -> none
    reduce_scatter x0 -> x1, waiting for transfers between devices: none -> 13.6 us  [per_device(): lax.psum_scatter(part, 'dp', scatter_dimension=1, tiled=True)]
    unnamed x18 -> x16, local copies, waits for them, and re-layouts: 4.59 us -> 16.7 us
  transfers between devices with their start and end apart: 17 -> 5, of which waited for: 17 -> 5; matrix products, arithmetic and copies ran while one was open for 8% -> 9% of each run, Pallas kernels for 0% -> 0%
where the time goes in v1:
time: 283 us
  waiting for transfers between devices  168 us (59%)
  blocking collectives  52.6 us (19%)
  matrix products  25.2 us (9%)
  local copies, waits for them, and re-layouts  16.9 us (6%)
  between operations  13.9 us (5%)
  other arithmetic  5.58 us (2%)
    unnamed x7, waiting for transfers between devices  88.9 us
    all_gather x1, waiting for transfers between devices, per_device(): all_gate = lax.all_gather(back_gate, 'blk', axis=0, tiled=True)  34.1 us
    all_gather x1, waiting for transfers between devices, per_device(): all_up = lax.all_gather(back_up, 'blk', axis=0, tiled=True)  31.9 us
    unnamed x16, local copies, waits for them, and re-layouts  16.7 us
    all_to_all x1, blocking collectives, per_device(): lax.all_to_all(normed, 'blk', split_axis=1, concat_axis=0, tiled=True)  16.1 us
    all_to_all x1, blocking collectives, per_device(): lax.all_to_all(part.astype(jnp.bfloat16), 'blk', split_axis=0, concat_axi...  14.4 us
    reduce_scatter x1, waiting for transfers between devices, per_device(): lax.psum_scatter(part, 'dp', scatter_dimension=1, tiled=True)  13.6 us
    psum x1, blocking collectives, per_device(): grad_gain = lax.psum(jnp.sum(own_sums * unit_slice, axis=0), 'blk')  12.4 us
  transfers between devices with their start and end apart: 5, of which 5 were waited for; matrix products, arithmetic and copies ran while one was open for 9% of the time, Pallas kernels for 0%

profile of v1, /device:TPU:0, one launch (start us, length us, event | category | flops | bytes accessed | tf_op | source)
XLA Modules:
  0.0 282.7 jit_solution(18118317254783270992)
XLA Ops:
  7.2 0.0 copy-start
  7.2 0.0 copy-start.3
  7.2 0.0 reduce-scatter.10.cloned.1.call-start
  7.2 1.5 copy.15
  8.7 0.4 fusion.1
  9.1 0.0 copy-done.3
  9.1 0.4 convert_divide_fusion
  9.5 16.1 %all_to_all.38 = bf16[128,8,320]{0,2,1:T(8,128)(2,1)S(1)} all-to-all(bf16[128,8,320]{0,2,1:T(8,128)(2,1)S(1)} %bitcast.44), channel_id=1, replica_groups=mesh['blk'=8,'dp'=4] {'blk'}, dimensions={1} | all-to-all | bytes 1310720 | tf_op jit(solution)/shard_map/all_to_all | solution.py:12
  25.6 0.0 copy-done
  25.6 0.0 copy-start.1
  25.6 3.8 %convolution_convert_fusion.1 = bf16[1024,1728]{0,1:T(8,128)(2,1)} fusion(bf16[320,1728]{1,0:T(8,128)(2,1)S(1)} %copy-done, bf16[128,8,320]{0,2,1:T(8,128)(2,1)S(1)} %all_to_all.38), kind=kOutput, calls=%fused_computation.1 | convolution fusion | flops 1134231552 | bytes 5300224 | tf_op jit(solution)/shard_map/dot_general | solution.py:13
  29.5 5.9 %copy.19 = bf16[1024,1728]{1,0:T(8,128)(2,1)} copy(bf16[1024,1728]{0,1:T(8,128)(2,1)} %convolution_convert_fusion.1) | data formatting | bytes 7077888
  35.3 0.0 reduce-scatter.10.cloned.1.call-update
  35.4 0.0 reduce-scatter.12.cloned.1.call-start
  35.4 0.0 copy-done.1
  35.4 5.2 %convolution_convert_fusion = bf16[1024,1728]{0,1:T(8,128)(2,1)} fusion(bf16[320,1728]{1,0:T(8,128)(2,1)} %param.8, bf16[128,8,320]{0,2,1:T(8,128)(2,1)S(1)} %all_to_all.38), kind=kOutput, calls=%fused_computation | convolution fusion | flops 1134231552 | bytes 5300224 | tf_op jit(solution)/shard_map/dot_general | solution.py:14
  40.6 6.0 %copy.21 = bf16[1024,1728]{1,0:T(8,128)(2,1)} copy(bf16[1024,1728]{0,1:T(8,128)(2,1)} %convolution_convert_fusion) | data formatting | bytes 7077888
  46.5 0.0 reduce-scatter.12.cloned.1.call-update
  46.6 0.0 all-gather.3.cloned.1.call-start
  46.6 37.0 %reduce-scatter.10.cloned.1.call-done = bf16[128,1728]{1,0:T(8,128)(2,1)} async-done(((bf16[1024,1728]{1,0:T(8,128)(2,1)}), bf16[128,1728]{1,0:T(8,128)(2,1)}) %reduce-scatter.10.cloned.1.call-update) | async-done | bytes 442384
  83.6 1.3 copy.20
  84.9 51.3 %reduce-scatter.12.cloned.1.call-done = bf16[128,1728]{1,0:T(8,128)(2,1)} async-done(((bf16[1024,1728]{1,0:T(8,128)(2,1)}), bf16[128,1728]{1,0:T(8,128)(2,1)}) %reduce-scatter.12.cloned.1.call-update) | async-done | bytes 442384
  136.2 1.3 copy.22
  137.5 2.6 fusion.7
  140.0 0.0 all-gather.3.cloned.1.call-update
  140.0 0.0 all-gather.5.cloned.1.call-start
  140.1 0.5 all-gather.5.cloned.1.call-update
  140.6 0.0 reduce-scatter.8.cloned.1.call-start
  140.7 34.1 %all-gather.3.cloned.1.call-done = bf16[1024,1728]{0,1:T(8,128)(2,1)} async-done(((bf16[128,1728]{0,1:T(8,128)(2,1)}), bf16[1024,1728]{0,1:T(8,128)(2,1)}) %all-gather.3.cloned.1.call-update) | async-done | bytes 3538960 | tf_op jit(solution)/shard_map/all_gather | solution.py:26
  174.7 4.4 %fusion.28 = f32[1024,320]{0,1:T(8,128)} fusion(bf16[320,1728]{1,0:T(8,128)(2,1)S(1)} %copy-done, bf16[1024,1728]{0,1:T(8,128)(2,1)} %all-gather.3.cloned.1.call-done), kind=kOutput, calls=%fused_computation.45 | convolution fusion | flops 1132462080 | bytes 5955584 | tf_op jit(solution)/shard_map/dot_general | solution.py:31
  179.1 31.9 %all-gather.5.cloned.1.call-done = bf16[1024,1728]{0,1:T(8,128)(2,1)} async-done(((bf16[128,1728]{0,1:T(8,128)(2,1)}), bf16[1024,1728]{0,1:T(8,128)(2,1)}) %all-gather.5.cloned.1.call-update) | async-done | bytes 3538960 | tf_op jit(solution)/shard_map/all_gather | solution.py:25
  211.0 4.1 %fusion.2 = bf16[40,8,8,128]{3,2,1,0:T(8,128)(2,1)S(1)} fusion(f32[1024,320]{0,1:T(8,128)} %fusion.28, bf16[320,1728]{1,0:T(8,128)(2,1)} %param.8, bf16[1024,1728]{0,1:T(8,128)(2,1)} %all-gather.5.cloned.1.call-done), kind=kOutput, calls=%fused_computation.11 | convolution fusion | flops 1133117440 | bytes 6610944 | tf_op jit(solution)/shard_map/dot_general | solution.py:33
  215.1 0.1 copy.42
  215.3 0.0 copy-start.2
  215.3 14.4 %all_to_all.39 = bf16[8,128,320]{1,2,0:T(8,128)(2,1)} all-to-all(bf16[8,128,320]{1,2,0:T(8,128)(2,1)S(1)} %bitcast.43), channel_id=1, replica_groups=mesh['blk'=8,'dp'=4] {'blk'}, dimensions={0} | all-to-all | bytes 1310720 | tf_op jit(solution)/shard_map/all_to_all | solution.py:34
  229.6 0.0 reduce-scatter.8.cloned.1.call-update
  229.7 0.1 dynamic_slice.6
  229.7 0.0 copy-done.2
  229.7 0.0 copy-start.4
  229.7 4.9 %fusion.12 = f32[320,1728]{1,0:T(8,128)} fusion(bf16[1024,1728]{0,1:T(8,128)(2,1)} %all-gather.5.cloned.1.call-done, bf16[128,8,320]{0,2,1:T(8,128)(2,1)S(1)} %copy-done.2), kind=kOutput, calls=%fused_computation.24 | convolution fusion | flops 1132462080 | bytes 6406144 | tf_op jit(solution)/shard_map/dot_general | solution.py:29
  234.7 0.0 copy-done.4
  234.7 2.8 fusion.14
  237.5 13.6 %reduce-scatter.8.cloned.1.call-done = bf16[128,640]{0,1:T(8,128)(2,1)} async-done(((bf16[128,2560]{0,1:T(8,128)(2,1)}), bf16[128,640]{0,1:T(8,128)(2,1)}) %reduce-scatter.8.cloned.1.call-update) | async-done | bytes 163856 | tf_op jit(solution)/shard_map/reduce_scatter | solution.py:41
  251.0 1.2 fusion.27
  252.2 9.7 %psum.14 = f32[128]{0:T(128)S(1)} all-reduce(f32[128]{0:T(128)S(1)} %get-tuple-element.16), channel_id=1, replica_groups=mesh['blk'=8,'dp'=4] {'dp'}, use_global_device_ids=true, to_apply=%region_5.0 | all-reduce | flops 128 | bytes 1024 | tf_op jit(solution)/shard_map/psum | solution.py:42
  261.9 1.1 fusion.26
  263.0 0.8 copy.18
  263.8 12.4 %psum.15 = f32[640]{0:T(1024)} all-reduce(f32[640]{0:T(1024)S(1)} %get-tuple-element.15), channel_id=1, replica_groups=mesh['blk'=8,'dp'=4] {'blk'}, use_global_device_ids=true, to_apply=%region_7.0 | all-reduce | flops 640 | bytes 5120 | tf_op jit(solution)/shard_map/psum | solution.py:47
  (2 shorter events, 0.0 us)
Async XLA Ops:
  7.2 18.5 %copy-start = (bf16[320,1728]{1,0:T(8,128)(2,1)S(1)}, bf16[320,1728]{1,0:T(8,128)(2,1)}, u32[]{:S(2)}) copy-start(bf16[320,1728]{1,0:T(8,128)(2,1)} %param.7) | copy-start | bytes 3317764
  7.2 1.9 copy-start.3
  7.2 76.4 %reduce-scatter.10.cloned.1.call-start = ((), (), s32[]{:S(2)}) async-start(), calls=%async_computation.8 | async-start | bytes 4128768
  25.6 9.8 %copy-start.1 = (bf16[128,8,320]{0,2,1:T(8,128)(2,1)}, bf16[128,8,320]{0,2,1:T(8,128)(2,1)S(1)}, u32[]{:S(2)}) copy-start(bf16[128,8,320]{0,2,1:T(8,128)(2,1)S(1)} %all_to_all.38) | copy-start | bytes 1966084
  35.4 100.8 %reduce-scatter.12.cloned.1.call-start = ((), (), s32[]{:S(2)}) async-start(), calls=%async_computation.9 | async-start | bytes 4128768
  46.6 128.2 %all-gather.3.cloned.1.call-start = ((), (), s32[]{:S(2)}) async-start(), calls=%async_computation.5 | async-start | bytes 3981312 | tf_op jit(solution)/shard_map/all_gather | solution.py:26
  140.0 71.0 %all-gather.5.cloned.1.call-start = ((), (), s32[]{:S(2)}) async-start(), calls=%async_computation.6 | async-start | bytes 3981312 | tf_op jit(solution)/shard_map/all_gather | solution.py:25
  140.6 110.4 %reduce-scatter.8.cloned.1.call-start = ((), (), s32[]{:S(2)}) async-start(), calls=%async_computation.7 | async-start | bytes 819200 | tf_op jit(solution)/shard_map/reduce_scatter | solution.py:41
  215.3 14.5 %copy-start.2 = (bf16[128,8,320]{0,2,1:T(8,128)(2,1)S(1)}, bf16[128,8,320]{0,2,1:T(8,128)(2,1)}, u32[]{:S(2)}) copy-start(bf16[128,8,320]{0,2,1:T(8,128)(2,1)} %copy-done.1) | copy-start | bytes 1966084
  229.7 4.9 %copy-start.4 = (bf16[1024,1728]{0,1:T(8,128)(2,1)S(1)}, bf16[1024,1728]{0,1:T(8,128)(2,1)}, u32[]{:S(2)}) copy-start(bf16[1024,1728]{0,1:T(8,128)(2,1)} %all-gather.3.cloned.1.call-done) | copy-start | bytes 10616836
Sparse Core Ops, SparseCore 0:
  35.5 48.0 reduce-scatter.9
  87.4 48.6 reduce-scatter.11
  140.2 34.5 all-gather.2
  176.5 34.5 all-gather.4
  229.8 21.2 reduce-scatter.7

commit v2 on v1

--- a/solution.py
+++ b/solution.py
@@ -1,10 +1,381 @@
+import functools
+
 import jax
 import jax.numpy as jnp
 from jax import lax
+from jax.experimental import pallas as pl
+from jax.experimental.pallas import tpu as pltpu
 from jax.sharding import PartitionSpec as P
 
-
-def per_device(inputs, gain, w_gate, w_up, upstream):
+MESH = pl.DeviceIdType.MESH
+ROWS = 16
+TILE = 256
+DIAG, ACROSS_X, ACROSS_Y, OWN = 6, 2, 4, 0
+DIRECTION = (ACROSS_X, ACROSS_Y)
+
+
+def plane_kernel(
+    dp, x_ref, gain_ref, wg_ref, wu_ref, up_ref,
+    hid_ref, gg_ref, gu_ref, gi_ref, ggain_ref,
+    nb, un, rm, xs, xt, pb, rc, sbuf, rbuf, full, ps, pr, zr, dots, dotr, gsum, gsend,
+    x_s, x_r, c_s, c_r, r_s, r_r, g_s, g_r, p_s, p_r, z_s, z_r, d_s, d_r, e_s, e_r,
+):
+    b, z = lax.axis_index("blk"), lax.axis_index("dp")
+    core, px, py = b % 2, (b // 2) % 2, b // 4
+    tokens, model = x_ref.shape
+    block = wg_ref.shape[0]
+    hidden = wg_ref.shape[1]
+    per = 8 // dp
+    weights = (wg_ref, wu_ref)
+    tiles = [(lo, min(TILE, hidden - lo)) for lo in range(0, hidden, TILE)]
+
+    def at(mask):
+        return (
+            b
+            + (1 - 2 * core) * (mask % 2)
+            + (2 - 4 * px) * ((mask // 2) % 2)
+            + (4 - 8 * py) * (mask // 4)
+        )
+
+    def chip_start(mask):
+        return at(mask) - core
+
+    def remote(src, dst, send, recv, mask):
+        return pltpu.make_async_remote_copy(
+            src_ref=src, dst_ref=dst, send_sem=send, recv_sem=recv,
+            device_id={"blk": at(mask)}, device_id_type=MESH,
+        )
+
+    def row_loop(body):
+        def step(i, carry):
+            body(pl.ds(pl.multiple_of(i * ROWS, ROWS), ROWS))
+            return carry
+
+        lax.fori_loop(0, tokens // ROWS, step, 0)
+
+    barrier = pltpu.get_barrier_semaphore()
+    for mask in range(1, 8):
+        pl.semaphore_signal(barrier, inc=1, device_id={"blk": at(mask)}, device_id_type=MESH)
+    for r in range(1, dp):
+        pl.semaphore_signal(
+            barrier, inc=1, device_id={"dp": (z + r) % dp}, device_id_type=MESH
+        )
+
+    def norm_rows(rows):
+        wide = x_ref[rows, :].astype(jnp.float32)
+        root = jnp.sqrt(jnp.mean(wide * wide, axis=1, keepdims=True) + 1e-05)
+        rm[rows, :] = jnp.broadcast_to(root, (ROWS, 128))
+        unit = wide / root
+        for j in range(8):
+            piece = unit[:, j * block : (j + 1) * block]
+            un[j, rows, :] = piece
+            nb[j, rows, :] = (piece * gain_ref[j]).astype(jnp.bfloat16)
+
+    row_loop(norm_rows)
+    pl.semaphore_wait(barrier, 7 + dp - 1)
+
+    x_copies = {}
+    for mask in (6, 7, 2, 3, 4, 5, 1):
+        copy = remote(nb.at[at(mask)], xs.at[b], x_s.at[mask], x_r.at[mask], mask)
+        copy.start()
+        x_copies[mask] = copy
+    xs[b] = nb[b]
+
+    def columns(mask):
+        return xs[pl.ds(chip_start(mask), 2)].reshape(2 * tokens, block)
+
+    def x_arrived(mask):
+        for m in (mask, mask + 1):
+            if m:
+                remote(nb.at[b], xs.at[at(m)], x_s.at[m], x_r.at[m], m).wait_recv()
+
+    slot = {DIAG: 0, ACROSS_X: 1, ACROSS_Y: 2, OWN: 3}
+    c_copies = {}
+
+    def forward(mask, mat):
+        k = slot[mask]
+        lhs = columns(mask)
+        for lo, width in tiles:
+            out = jnp.dot(
+                lhs, weights[mat][:, lo : lo + width], preferred_element_type=jnp.float32
+            )
+            pb[k, mat, :, :, lo : lo + width] = out.astype(jnp.bfloat16).reshape(
+                2, tokens, width
+            )
+        copy = remote(pb.at[k, mat, 1 - core], rc.at[k, mat], c_s.at[k, mat], c_r.at[k, mat], 1)
+        copy.start()
+        c_copies[k, mat] = copy
+
+    r_copies = {}
+
+    def send_sum(mask, mat, e, to, extra=None):
+        k = slot[mask]
+        c_copies[k, mat].wait_recv()
+        if extra is not None:
+            r_copies[mat, extra].wait_recv()
+
+        def rows_sum(rows):
+            total = pb[k, mat, core, rows, :].astype(jnp.float32) + rc[k, mat, rows, :].astype(
+                jnp.float32
+            )
+            if extra is not None:
+                total = total + rbuf[mat, extra, rows, :].astype(jnp.float32)
+            sbuf[mat, e, rows, :] = total.astype(jnp.bfloat16)
+
+        row_loop(rows_sum)
+        copy = remote(sbuf.at[mat, e], rbuf.at[mat, e], r_s.at[mat, e], r_r.at[mat, e], to)
+        copy.start()
+        r_copies[mat, e] = copy
+
+    x_arrived(DIAG)
+    forward(DIAG, 0)
+    forward(DIAG, 1)
+    x_arrived(ACROSS_X)
+    forward(ACROSS_X, 0)
+    send_sum(DIAG, 0, 0, ACROSS_X)
+    send_sum(DIAG, 1, 0, ACROSS_Y)
+    x_arrived(ACROSS_Y)
+    forward(ACROSS_Y, 1)
+    send_sum(ACROSS_X, 0, 1, ACROSS_X)
+    send_sum(ACROSS_Y, 1, 1, ACROSS_Y)
+    forward(ACROSS_Y, 0)
+    forward(ACROSS_X, 1)
+    x_arrived(OWN)
+    forward(OWN, 0)
+    forward(OWN, 1)
+    for mask in (OWN, ACROSS_X, ACROSS_Y, DIAG):
+        xt[slot[mask]] = columns(mask).T
+    send_sum(ACROSS_Y, 0, 2, ACROSS_Y, extra=0)
+    send_sum(ACROSS_X, 1, 2, ACROSS_X, extra=0)
+    for mat in (0, 1):
+        c_copies[3, mat].wait_recv()
+        r_copies[mat, 1].wait_recv()
+        r_copies[mat, 2].wait_recv()
+
+    def act_rows(rows):
+        pre = []
+        for mat in (0, 1):
+            total = pb[3, mat, core, rows, :].astype(jnp.float32) + rc[3, mat, rows, :].astype(
+                jnp.float32
+            )
+            total = total + rbuf[mat, 1, rows, :].astype(jnp.float32)
+            pre.append(total + rbuf[mat, 2, rows, :].astype(jnp.float32))
+        gate_pre, up_pre = pre
+        sig = jax.nn.sigmoid(gate_pre)
+        activated = gate_pre * sig
+        hid_ref[rows, :] = (activated * up_pre).astype(jnp.bfloat16)
+        wide = up_ref[rows, :].astype(jnp.float32)
+        full[1, b, rows, :] = (wide * activated).astype(jnp.bfloat16)
+        full[0, b, rows, :] = (
+            wide * up_pre * sig * (1.0 + gate_pre * (1.0 - sig))
+        ).astype(jnp.bfloat16)
+
+    row_loop(act_rows)
+
+    g_sends = []
+
+    def pass_on(mat, origin, to):
+        there = origin ^ to
+        t = at(origin)
+        copy = remote(
+            full.at[mat, t], full.at[mat, t], g_s.at[mat, there], g_r.at[mat, there], to
+        )
+        copy.start()
+        g_sends.append(copy)
+
+    def arrived(mat, origin):
+        t = at(origin)
+        remote(
+            full.at[mat, t], full.at[mat, t], g_s.at[mat, origin], g_r.at[mat, origin], 1
+        ).wait_recv()
+
+    pass_on(0, OWN, ACROSS_X)
+    pass_on(1, OWN, ACROSS_Y)
+    pass_on(0, OWN, 1)
+    pass_on(1, OWN, 1)
+    pass_on(1, OWN, ACROSS_X)
+    pass_on(0, OWN, ACROSS_Y)
+
+    p_copies = {}
+
+    def back(mask, first):
+        k = slot[mask]
+        start = chip_start(mask)
+        grads = []
+        for mat, out_ref in ((0, gg_ref), (1, gu_ref)):
+            for lo, width in tiles:
+                piece = full[mat, pl.ds(start, 2), :, lo : lo + width].reshape(2 * tokens, width)
+                term = jnp.dot(xt[k], piece, preferred_element_type=jnp.float32)
+                if first:
+                    out_ref[:, lo : lo + width] = term
+                else:
+                    out_ref[:, lo : lo + width] += term
+            grads.append(
+                lax.dot_general(
+                    full[mat, pl.ds(start, 2)].reshape(2 * tokens, hidden),
+                    weights[mat][...],
+                    (((1,), (1,)), ((), ())),
+                    preferred_element_type=jnp.float32,
+                )
+            )
+        ps[pl.ds(start, 2)] = (grads[0] + grads[1]).astype(jnp.bfloat16).reshape(2, tokens, block)
+        for m in (mask, mask + 1):
+            if m:
+                copy = remote(ps.at[at(m)], pr.at[b], p_s.at[m], p_r.at[m], m)
+                copy.start()
+                p_copies[m] = copy
+            else:
+                pr[b] = ps[b]
+
+    arrived(0, 1)
+    arrived(1, 1)
+    back(OWN, True)
+    arrived(0, ACROSS_X)
+    pass_on(0, ACROSS_X, ACROSS_Y)
+    pass_on(0, ACROSS_X, 1)
+    arrived(1, ACROSS_Y)
+    pass_on(1, ACROSS_Y, ACROSS_X)
+    pass_on(1, ACROSS_Y, 1)
+    arrived(1, ACROSS_X)
+    pass_on(1, ACROSS_X, 1)
+    arrived(0, ACROSS_Y)
+    pass_on(0, ACROSS_Y, 1)
+    arrived(0, ACROSS_X + 1)
+    arrived(1, ACROSS_X + 1)
+    back(ACROSS_X, False)
+    arrived(0, ACROSS_Y + 1)
+    arrived(1, ACROSS_Y + 1)
+    back(ACROSS_Y, False)
+    arrived(0, DIAG)
+    pass_on(0, DIAG, 1)
+    arrived(1, DIAG)
+    pass_on(1, DIAG, 1)
+    arrived(0, DIAG + 1)
+    arrived(1, DIAG + 1)
+    back(DIAG, False)
+
+    for m in range(1, 8):
+        remote(ps.at[b], pr.at[at(m)], p_s.at[m], p_r.at[m], m).wait_recv()
+
+    def over_dp(src, dst, send, recv, r):
+        return pltpu.make_async_remote_copy(
+            src_ref=src, dst_ref=dst, send_sem=send, recv_sem=recv,
+            device_id={"dp": (z + r) % dp}, device_id_type=MESH,
+        )
+
+    z_copies = []
+    for r in range(1, dp):
+        to = (z + r) % dp
+        copy = over_dp(pr.at[pl.ds(to * per, per)], zr.at[z], z_s.at[r], z_r.at[r], r)
+        copy.start()
+        z_copies.append(copy)
+
+    dot = jnp.zeros((tokens, 1), jnp.float32)
+    for j in range(8):
+        dot = dot + jnp.sum(
+            pr[j].astype(jnp.float32) * gain_ref[j] * un[j], axis=1, keepdims=True
+        )
+    dots[...] = jnp.broadcast_to(dot, (tokens, tokens)).T[0:8, :]
+    for r in range(1, dp):
+        copy = over_dp(dots, dotr.at[z], d_s.at[r], d_r.at[r], r)
+        copy.start()
+        z_copies.append(copy)
+    for r in range(1, dp):
+        source = (z + dp - r) % dp
+        over_dp(pr.at[pl.ds(0, per)], zr.at[source], z_s.at[r], z_r.at[r], r).wait_recv()
+    sums = []
+    for jj in range(per):
+        j = z * per + jj
+        total = pr[j].astype(jnp.float32)
+        for r in range(1, dp):
+            total = total + zr[(z + r) % dp, jj].astype(jnp.float32)
+        sums.append(total)
+        part = jnp.sum(total * un[j], axis=0, keepdims=True)
+        gsend[:, jj, :] = jnp.broadcast_to(part, (8, block))
+    e_copies = []
+    for m in range(1, 8):
+        copy = remote(gsend, gsum.at[b], e_s.at[m], e_r.at[m], m)
+        copy.start()
+        e_copies.append(copy)
+    total_dot = dots[...]
+    for r in range(1, dp):
+        source = (z + dp - r) % dp
+        over_dp(dots, dotr.at[source], d_s.at[r], d_r.at[r], r).wait_recv()
+        total_dot = total_dot + dotr[source]
+    means = jnp.broadcast_to(total_dot[0:1, :] / model, (tokens, tokens)).T[:, 0:1]
+    root = rm[:, 0:1]
+    for jj in range(per):
+        j = z * per + jj
+        value = (sums[jj] * gain_ref[j] - un[j] * means) / root
+        gi_ref[:, jj * block : (jj + 1) * block] = value.astype(jnp.bfloat16)
+    total_gain = gsend[...]
+    for m in range(1, 8):
+        remote(gsend, gsum.at[at(m)], e_s.at[m], e_r.at[m], m).wait_recv()
+        total_gain = total_gain + gsum[at(m)]
+    ggain_ref[...] = total_gain[0]
+
+    for group in (x_copies, c_copies, r_copies, p_copies):
+        for copy in group.values():
+            copy.wait_send()
+    for copy in g_sends + z_copies + e_copies:
+        copy.wait_send()
+
+
+def by_kernel(dp, inputs, gain, w_gate, w_up, upstream):
+    tokens, model = inputs.shape
+    block, hidden = w_gate.shape
+    per = 8 // dp
+    bf16, f32 = jnp.bfloat16, jnp.float32
+    vmem = pl.BlockSpec(memory_space=pltpu.VMEM)
+
+    def dma(*shape):
+        return pltpu.SemaphoreType.DMA(shape)
+
+    hid, grad_gate, grad_up, grad_input, grad_gain = pl.pallas_call(
+        functools.partial(plane_kernel, dp),
+        out_shape=(
+            jax.ShapeDtypeStruct((tokens, hidden), bf16),
+            jax.ShapeDtypeStruct((block, hidden), f32),
+            jax.ShapeDtypeStruct((block, hidden), f32),
+            jax.ShapeDtypeStruct((tokens, per * block), bf16),
+            jax.ShapeDtypeStruct((per, block), f32),
+        ),
+        in_specs=[vmem] * 5,
+        out_specs=(vmem,) * 5,
+        scratch_shapes=[
+            pltpu.VMEM((8, tokens, block), bf16),
+            pltpu.VMEM((8, tokens, block), f32),
+            pltpu.VMEM((tokens, 128), f32),
+            pltpu.VMEM((8, tokens, block), bf16),
+            pltpu.VMEM((4, block, 2 * tokens), bf16),
+            pltpu.VMEM((4, 2, 2, tokens, hidden), bf16),
+            pltpu.VMEM((4, 2, tokens, hidden), bf16),
+            pltpu.VMEM((2, 3, tokens, hidden), bf16),
+            pltpu.VMEM((2, 3, tokens, hidden), bf16),
+            pltpu.VMEM((2, 8, tokens, hidden), bf16),
+            pltpu.VMEM((8, tokens, block), bf16),
+            pltpu.VMEM((8, tokens, block), bf16),
+            pltpu.VMEM((dp, per, tokens, block), bf16),
+            pltpu.VMEM((8, tokens), f32),
+            pltpu.VMEM((dp, 8, tokens), f32),
+            pltpu.VMEM((8, 8, per, block), f32),
+            pltpu.VMEM((8, per, block), f32),
+            dma(8), dma(8), dma(4, 2), dma(4, 2), dma(2, 3), dma(2, 3), dma(2, 8), dma(2, 8),
+            dma(8), dma(8), dma(dp), dma(dp), dma(dp), dma(dp), dma(8), dma(8),
+        ],
+        compiler_params=pltpu.CompilerParams(
+            collective_id=0, has_side_effects=True, vmem_limit_bytes=60 * 2**20
+        ),
+        cost_estimate=pl.CostEstimate(
+            flops=48 * tokens * block * hidden * 2,
+            bytes_accessed=16 * block * hidden,
+            transcendentals=tokens * hidden,
+        ),
+    )(inputs, gain.reshape(8, 1, block), w_gate, w_up, upstream)
+    return hid, grad_gate, grad_up, grad_input, grad_gain.reshape(per * block)
+
+
+def by_collectives(inputs, gain, w_gate, w_up, upstream):
     wide_input = inputs.astype(jnp.float32)
     root_mean = jnp.sqrt(jnp.mean(wide_input * wide_input, axis=1, keepdims=True) + 1e-05)
     unit_input = wide_input / root_mean
@@ -49,8 +420,10 @@
 
 
 def solution(mesh):
+    dp = mesh.shape["dp"]
+    by_chip = mesh.shape["blk"] == 8 and 8 % dp == 0
     return jax.shard_map(
-        per_device,
+        functools.partial(by_kernel, dp) if by_chip else by_collectives,
         mesh=mesh,
         in_specs=(P("blk", None), P(), P("blk", "dp"), P("blk", "dp"), P("blk", "dp")),
         out_specs=(P("blk", "dp"), P("blk", "dp"), P("blk", "dp"), P("blk", "dp"), P("dp")),

time: 283 us -> 129 us (0.46)
  waiting for transfers between devices: 168 us -> 0 us
  Pallas kernels: 0 us -> 115 us
  blocking collectives: 52.6 us -> 0 us
  matrix products: 25.2 us -> 0 us
  between operations: 13.9 us -> 0.64 us
  other arithmetic: 5.58 us -> 0 us
  local copies, waits for them, and re-layouts: 16.9 us -> 12.1 us
    pallas_call x0 -> x1, Pallas kernels: none -> 115 us  [by_kernel(): pl.pallas_call(functools.partial(plane_kernel, dp), out_shape=(jax.ShapeD...]
    unnamed x7 -> x0, waiting for transfers between devices: 88.9 us -> none
    all_gather x2 -> x0, waiting for transfers between devices: 66 us -> none  [the longest x1 34.1 us: per_device(): all_gate = lax.all_gather(back_gate, 'blk', axis=0, tiled=True)]
    all_to_all x2 -> x0, blocking collectives: 30.5 us -> none  [the longest x1 16.1 us: per_device(): lax.all_to_all(normed, 'blk', split_axis=1, concat_axis=0, tiled=True)]
    dot_general x6 -> x0, matrix products: 25.2 us -> none  [the longest x1 5.17 us: per_device(): jnp.dot(columns, w_up, preferred_element_type=jnp.float32)]
    psum x2 -> x0, blocking collectives: 22.1 us -> none  [the longest x1 12.4 us: per_device(): grad_gain = lax.psum(jnp.sum(own_sums * unit_slice, axis=0), 'blk')]
    reduce_scatter x1 -> x0, waiting for transfers between devices: 13.6 us -> none  [per_device(): lax.psum_scatter(part, 'dp', scatter_dimension=1, tiled=True)]
    unnamed x16 -> x9, local copies, waits for them, and re-layouts: 16.7 us -> 9.35 us
  transfers between devices with their start and end apart: 5 -> 0, of which waited for: 5 -> 0; matrix products, arithmetic and copies ran while one was open for 9% -> 0% of each run, Pallas kernels for 0% -> 0%
where the time goes in v2:
time: 129 us; the launch traced here: 127 us
  Pallas kernels  115 us (89%)
  local copies, waits for them, and re-layouts  12.1 us (9%)
    pallas_call x1, Pallas kernels, by_kernel(): pl.pallas_call(functools.partial(plane_kernel, dp), out_shape=(jax.ShapeD...  115 us
    unnamed x9, local copies, waits for them, and re-layouts  9.35 us

profile of v2, /device:TPU:0, one launch (start us, length us, event | category | flops | bytes accessed | tf_op | source)
XLA Modules:
  0.0 127.4 jit_solution(17298762833060574801)
XLA Ops:
  0.6 1.4 %reshape.16.gain_ref = f32[8,1,320]{2,1,0:T(1,128)} reshape(f32[2560]{0:T(1024)} %param.6) | data formatting | bytes 20480 | tf_op jit(solution)/shard_map/reshape | solution.py:374
  2.0 2.0 %copy.10.up_ref = bf16[128,1728]{1,0:T(8,128)(2,1)} copy(bf16[128,1728]{0,1:T(8,128)(2,1)} %param.9) | data formatting | bytes 884736 | tf_op args[4]
  4.0 114.7 %shard_map.92 = (bf16[128,1728]{1,0:T(8,128)(2,1)}, f32[320,1728]{1,0:T(8,128)}, f32[320,1728]{1,0:T(8,128)}, bf16[128,640]{1,0:T(8,128)(2,1)}, f32[2,320]{1,0:T(2,128)}) custom-call(bf16[128,2560]{1,0:T(8,128)(2,1)} %x_ref.1, f32[8,1,320]{2,1,0:T(1,128)} %reshape.16.gain_ref, bf16[320,1728]{1,0:T(8,128)(2,1)} %wg_ref.1, bf16[320,1728]{1,0:T(8,128)(2,1)} %wu_ref.1, ...), custom_call_target="tpu_custom_call" | custom-call | flops 6794772480 | bytes 8847360 | tf_op jit(solution)/shard_map/pallas_call | solution.py:334
  118.7 2.0 %copy.11 = bf16[128,1728]{0,1:T(8,128)(2,1)} copy(bf16[128,1728]{1,0:T(8,128)(2,1)} %get-tuple-element.15) | data formatting | bytes 884736
  120.7 1.3 %reshape.17 = f32[640]{0:T(1024)} reshape(f32[2,320]{1,0:T(2,128)} %get-tuple-element.14) | data formatting | bytes 5120 | tf_op jit(solution)/shard_map/reshape | solution.py:375
  122.0 0.0 copy-start
  122.0 3.3 %copy.15 = f32[320,1728]{1,0:T(8,128)} copy(f32[320,1728]{1,0:T(8,128)} %get-tuple-element.26) | data formatting | bytes 4423680
  125.4 0.0 copy-done
  125.4 0.0 copy-start.1
  125.4 1.4 %copy.16 = f32[320,1728]{1,0:T(8,128)} copy(f32[320,1728]{1,0:T(8,128)S(1)} %copy-done) | data formatting | bytes 4423680
  126.8 0.0 copy-done.1
  126.8 0.7 copy.17
Async XLA Ops:
  122.0 3.3 %copy-start = (f32[320,1728]{1,0:T(8,128)S(1)}, f32[320,1728]{1,0:T(8,128)}, u32[]{:S(2)}) copy-start(f32[320,1728]{1,0:T(8,128)} %get-tuple-element.27) | copy-start | bytes 6635524
  125.4 1.4 %copy-start.1 = (bf16[128,640]{1,0:T(8,128)(2,1)S(1)}, bf16[128,640]{1,0:T(8,128)(2,1)}, u32[]{:S(2)}) copy-start(bf16[128,640]{1,0:T(8,128)(2,1)} %get-tuple-element.28) | copy-start | bytes 491524

commit v3 on v1

--- a/solution.py
+++ b/solution.py
@@ -1,10 +1,496 @@
+import functools
+
 import jax
 import jax.numpy as jnp
 from jax import lax
+from jax.experimental import pallas as pl
+from jax.experimental.pallas import tpu as pltpu
 from jax.sharding import PartitionSpec as P
 
-
-def per_device(inputs, gain, w_gate, w_up, upstream):
+MESH = pl.DeviceIdType.MESH
+ROWS = 16
+TILE = 256
+DIAG, ACROSS_X, ACROSS_Y, OWN = 6, 2, 4, 0
+SLOT = {DIAG: 0, ACROSS_X: 1, ACROSS_Y: 2, OWN: 3}
+
+
+def chunks_of(hidden):
+    first = (hidden // TILE + 2) // 2 * TILE
+    return ((0, first), (first, hidden - first))
+
+
+def plane_kernel(
+    dp, x_ref, gain_ref, wg_ref, wu_ref, up_ref,
+    hid_ref, gg_ref, gu_ref, gi_ref, ggain_ref,
+    nb, un, gs, rm, xs, xt, wgs, wus, ggs, gus, hid, pacc, ps, pr, zr, dots, dotr, gsum, gsend,
+    ups0, hs0, pb0, rc0, sbuf0, rbuf0, full0,
+    ups1, hs1, pb1, rc1, sbuf1, rbuf1, full1,
+    x_s, x_r, c_s, c_r, r_s, r_r, g_s, g_r, p_s, p_r, z_s, z_r, d_s, d_r, e_s, e_r, l_s,
+):
+    b, z = lax.axis_index("blk"), lax.axis_index("dp")
+    core, px, py = b % 2, (b // 2) % 2, b // 4
+    tokens, model = x_ref.shape
+    block, hidden = wgs.shape
+    per = 8 // dp
+    weights = (wgs, wus)
+    chunks = chunks_of(hidden)
+    ups, hs, pb, rc = (ups0, ups1), (hs0, hs1), (pb0, pb1), (rc0, rc1)
+    sbuf, rbuf, full = (sbuf0, sbuf1), (rbuf0, rbuf1), (full0, full1)
+
+    def tiles(h):
+        width = chunks[h][1]
+        return [(lo, min(TILE, width - lo)) for lo in range(0, width, TILE)]
+
+    def at(mask):
+        return (
+            b
+            + (1 - 2 * core) * (mask % 2)
+            + (2 - 4 * px) * ((mask // 2) % 2)
+            + (4 - 8 * py) * (mask // 4)
+        )
+
+    def chip_start(mask):
+        return at(mask) - core
+
+    def remote(src, dst, send, recv, mask):
+        return pltpu.make_async_remote_copy(
+            src_ref=src, dst_ref=dst, send_sem=send, recv_sem=recv,
+            device_id={"blk": at(mask)}, device_id_type=MESH,
+        )
+
+    def over_dp(src, dst, send, recv, to):
+        return pltpu.make_async_remote_copy(
+            src_ref=src, dst_ref=dst, send_sem=send, recv_sem=recv,
+            device_id={"dp": to}, device_id_type=MESH,
+        )
+
+    def row_loop(body):
+        def step(i, carry):
+            body(pl.ds(pl.multiple_of(i * ROWS, ROWS), ROWS))
+            return carry
+
+        lax.fori_loop(0, tokens // ROWS, step, 0)
+
+    barrier = pltpu.get_barrier_semaphore()
+    for mask in range(1, 8):
+        pl.semaphore_signal(barrier, inc=1, device_id={"blk": at(mask)}, device_id_type=MESH)
+    for r in range(1, dp):
+        pl.semaphore_signal(
+            barrier, inc=1, device_id={"dp": (z + r) % dp}, device_id_type=MESH
+        )
+    loads = [
+        pltpu.make_async_copy(wg_ref, wgs, l_s.at[0]),
+        pltpu.make_async_copy(wu_ref, wus, l_s.at[1]),
+    ]
+    for copy in loads:
+        copy.start()
+    for j in range(8):
+        gs[j] = gain_ref[:, j * block : (j + 1) * block]
+
+    def norm_rows(rows):
+        wide = x_ref[rows, :].astype(jnp.float32)
+        root = jnp.sqrt(jnp.mean(wide * wide, axis=1, keepdims=True) + 1e-05)
+        rm[rows, :] = jnp.broadcast_to(root, (ROWS, 128))
+        unit = wide / root
+        for j in range(8):
+            piece = unit[:, j * block : (j + 1) * block]
+            un[j, rows, :] = piece
+            nb[j, rows, :] = (piece * gs[j]).astype(jnp.bfloat16)
+
+    row_loop(norm_rows)
+    pl.semaphore_wait(barrier, 7 + dp - 1)
+
+    sends = []
+
+    def start(copy):
+        copy.start()
+        sends.append(copy)
+        return copy
+
+    for mask in (6, 7, 2, 3, 4, 5, 1):
+        start(remote(nb.at[at(mask)], xs.at[b], x_s.at[mask], x_r.at[mask], mask))
+    xs[b] = nb[b]
+    for copy in loads:
+        copy.wait()
+
+    def columns(mask):
+        return xs[pl.ds(chip_start(mask), 2)].reshape(2 * tokens, block)
+
+    def x_arrived(mask):
+        for m in (mask, mask + 1):
+            if m:
+                remote(nb.at[b], xs.at[at(m)], x_s.at[m], x_r.at[m], m).wait_recv()
+
+    c_copies, r_copies = {}, {}
+
+    def forward(mask, mat, h):
+        k = SLOT[mask]
+        lhs = columns(mask)
+        base = chunks[h][0]
+        for lo, width in tiles(h):
+            out = jnp.dot(
+                lhs,
+                weights[mat][:, base + lo : base + lo + width],
+                preferred_element_type=jnp.float32,
+            )
+            pb[h][k, mat, :, :, lo : lo + width] = out.astype(jnp.bfloat16).reshape(
+                2, tokens, width
+            )
+        c_copies[k, mat, h] = start(
+            remote(
+                pb[h].at[k, mat, 1 - core], rc[h].at[k, mat],
+                c_s.at[h, k, mat], c_r.at[h, k, mat], 1,
+            )
+        )
+
+    def send_sum(mask, mat, e, to, h, extra=None):
+        k = SLOT[mask]
+        c_copies[k, mat, h].wait_recv()
+        if extra is not None:
+            r_copies[mat, extra, h].wait_recv()
+
+        def rows_sum(rows):
+            total = pb[h][k, mat, core, rows, :].astype(jnp.float32)
+            total = total + rc[h][k, mat, rows, :].astype(jnp.float32)
+            if extra is not None:
+                total = total + rbuf[h][mat, extra, rows, :].astype(jnp.float32)
+            sbuf[h][mat, e, rows, :] = total.astype(jnp.bfloat16)
+
+        row_loop(rows_sum)
+        r_copies[mat, e, h] = start(
+            remote(
+                sbuf[h].at[mat, e], rbuf[h].at[mat, e],
+                r_s.at[h, mat, e], r_r.at[h, mat, e], to,
+            )
+        )
+
+    def activate(h):
+        for mat in (0, 1):
+            c_copies[3, mat, h].wait_recv()
+            r_copies[mat, 1, h].wait_recv()
+            r_copies[mat, 2, h].wait_recv()
+
+        def act_rows(rows):
+            pre = []
+            for mat in (0, 1):
+                total = pb[h][3, mat, core, rows, :].astype(jnp.float32)
+                total = total + rc[h][3, mat, rows, :].astype(jnp.float32)
+                total = total + rbuf[h][mat, 1, rows, :].astype(jnp.float32)
+                pre.append(total + rbuf[h][mat, 2, rows, :].astype(jnp.float32))
+            gate_pre, up_pre = pre
+            sig = jax.nn.sigmoid(gate_pre)
+            activated = gate_pre * sig
+            hs[h][rows, :] = (activated * up_pre).astype(jnp.bfloat16)
+            wide = ups[h][rows, :].astype(jnp.float32)
+            full[h][1, b, rows, :] = (wide * activated).astype(jnp.bfloat16)
+            full[h][0, b, rows, :] = (
+                wide * up_pre * sig * (1.0 + gate_pre * (1.0 - sig))
+            ).astype(jnp.bfloat16)
+
+        row_loop(act_rows)
+        pass_on(0, OWN, ACROSS_X, h)
+        pass_on(1, OWN, ACROSS_Y, h)
+        pass_on(0, OWN, 1, h)
+        pass_on(1, OWN, 1, h)
+        pass_on(1, OWN, ACROSS_X, h)
+        pass_on(0, OWN, ACROSS_Y, h)
+
+    def pass_on(mat, origin, to, h):
+        there = origin ^ to
+        t = at(origin)
+        start(
+            remote(
+                full[h].at[mat, t], full[h].at[mat, t],
+                g_s.at[h, mat, there], g_r.at[h, mat, there], to,
+            )
+        )
+
+    def arrived(mat, origin, h):
+        t = at(origin)
+        remote(
+            full[h].at[mat, t], full[h].at[mat, t],
+            g_s.at[h, mat, origin], g_r.at[h, mat, origin], 1,
+        ).wait_recv()
+
+    def back_inputs(mask, h):
+        base, width = chunks[h]
+        first = chip_start(mask)
+        part = pacc[SLOT[mask]] if h else None
+        for mat in (0, 1):
+            term = lax.dot_general(
+                full[h][mat, pl.ds(first, 2)].reshape(2 * tokens, width),
+                weights[mat][:, base : base + width],
+                (((1,), (1,)), ((), ())),
+                preferred_element_type=jnp.float32,
+            )
+            part = term if part is None else part + term
+        if h == 0:
+            pacc[SLOT[mask]] = part
+            return
+        ps[pl.ds(first, 2)] = part.astype(jnp.bfloat16).reshape(2, tokens, block)
+        for m in (mask, mask + 1):
+            if m:
+                start(remote(ps.at[at(m)], pr.at[b], p_s.at[m], p_r.at[m], m))
+            else:
+                pr[b] = ps[b]
+
+    def back_weights(mask, h):
+        base = chunks[h][0]
+        for mat, out_ref in ((0, ggs), (1, gus)):
+            for lo, width in tiles(h):
+                piece = full[h][mat, pl.ds(chip_start(mask), 2), :, lo : lo + width]
+                term = jnp.dot(
+                    xt[SLOT[mask]],
+                    piece.reshape(2 * tokens, width),
+                    preferred_element_type=jnp.float32,
+                )
+                if mask == OWN:
+                    out_ref[:, base + lo : base + lo + width] = term
+                else:
+                    out_ref[:, base + lo : base + lo + width] += term
+
+    def forward_first(h):
+        arrived(0, ACROSS_X, h)
+        pass_on(0, ACROSS_X, ACROSS_Y, h)
+        pass_on(0, ACROSS_X, 1, h)
+        arrived(1, ACROSS_Y, h)
+        pass_on(1, ACROSS_Y, ACROSS_X, h)
+        pass_on(1, ACROSS_Y, 1, h)
+
+    def forward_second(h):
+        arrived(1, ACROSS_X, h)
+        pass_on(1, ACROSS_X, 1, h)
+        arrived(0, ACROSS_Y, h)
+        pass_on(0, ACROSS_Y, 1, h)
+
+    def forward_last(h):
+        arrived(1, DIAG, h)
+        pass_on(1, DIAG, 1, h)
+        arrived(0, DIAG, h)
+        pass_on(0, DIAG, 1, h)
+
+    def other_core(mask, h):
+        arrived(0, mask + 1, h)
+        arrived(1, mask + 1, h)
+
+    x_arrived(DIAG)
+    forward(DIAG, 0, 0)
+    forward(DIAG, 1, 0)
+    x_arrived(ACROSS_X)
+    forward(ACROSS_X, 0, 0)
+    send_sum(DIAG, 0, 0, ACROSS_X, 0)
+    send_sum(DIAG, 1, 0, ACROSS_Y, 0)
+    x_arrived(ACROSS_Y)
+    forward(ACROSS_Y, 1, 0)
+    send_sum(ACROSS_X, 0, 1, ACROSS_X, 0)
+    send_sum(ACROSS_Y, 1, 1, ACROSS_Y, 0)
+    forward(ACROSS_Y, 0, 0)
+    forward(ACROSS_X, 1, 0)
+    x_arrived(OWN)
+    forward(OWN, 0, 0)
+    forward(OWN, 1, 0)
+    forward(DIAG, 0, 1)
+    forward(DIAG, 1, 1)
+    for h, (base, width) in enumerate(chunks):
+        ups[h][...] = up_ref[base : base + width, :].T
+    send_sum(ACROSS_Y, 0, 2, ACROSS_Y, 0, extra=0)
+    send_sum(ACROSS_X, 1, 2, ACROSS_X, 0, extra=0)
+    send_sum(DIAG, 0, 0, ACROSS_X, 1)
+    send_sum(DIAG, 1, 0, ACROSS_Y, 1)
+    forward(ACROSS_X, 0, 1)
+    forward(ACROSS_Y, 1, 1)
+    forward(ACROSS_Y, 0, 1)
+    forward(ACROSS_X, 1, 1)
+    send_sum(ACROSS_X, 0, 1, ACROSS_X, 1)
+    send_sum(ACROSS_Y, 1, 1, ACROSS_Y, 1)
+    forward(OWN, 0, 1)
+    forward(OWN, 1, 1)
+    for mask in (OWN, ACROSS_X, ACROSS_Y, DIAG):
+        xt[SLOT[mask]] = columns(mask).T
+    activate(0)
+    send_sum(ACROSS_Y, 0, 2, ACROSS_Y, 1, extra=0)
+    send_sum(ACROSS_X, 1, 2, ACROSS_X, 1, extra=0)
+    hid[0 : chunks[0][1], :] = hs[0][...].T
+    forward_first(0)
+    activate(1)
+    other_core(OWN, 0)
+    back_inputs(OWN, 0)
+    back_weights(OWN, 0)
+    forward_second(0)
+    other_core(ACROSS_X, 0)
+    back_inputs(ACROSS_X, 0)
+    other_core(ACROSS_Y, 0)
+    back_inputs(ACROSS_Y, 0)
+    forward_last(0)
+    hid[chunks[1][0] : hidden, :] = hs[1][...].T
+    stores = [pltpu.make_async_copy(hid, hid_ref, l_s.at[2])]
+    stores[0].start()
+    back_weights(ACROSS_X, 0)
+    forward_first(1)
+    back_weights(ACROSS_Y, 0)
+    other_core(DIAG, 0)
+    back_inputs(DIAG, 0)
+    other_core(OWN, 1)
+    back_inputs(OWN, 1)
+    forward_second(1)
+    back_weights(DIAG, 0)
+
+    dot = [jnp.zeros((tokens, 1), jnp.float32)]
+
+    def collect(mask):
+        for m in (mask, mask + 1):
+            if m:
+                remote(ps.at[b], pr.at[at(m)], p_s.at[m], p_r.at[m], m).wait_recv()
+        first = chip_start(mask)
+        to = first // per
+
+        @pl.when(to != z)
+        def _():
+            r = (to - z + dp) % dp
+            over_dp(pr.at[pl.ds(first, per)], zr.at[z], z_s.at[r], z_r.at[r], to).start()
+
+        for c in range(2):
+            j = first + c
+            dot[0] = dot[0] + jnp.sum(
+                pr[j].astype(jnp.float32) * gs[j] * un[j], axis=1, keepdims=True
+            )
+
+    other_core(ACROSS_X, 1)
+    back_inputs(ACROSS_X, 1)
+    other_core(ACROSS_Y, 1)
+    back_inputs(ACROSS_Y, 1)
+    back_weights(OWN, 1)
+    collect(OWN)
+    forward_last(1)
+    back_weights(ACROSS_X, 1)
+    other_core(DIAG, 1)
+    back_inputs(DIAG, 1)
+    collect(ACROSS_X)
+    collect(ACROSS_Y)
+    back_weights(ACROSS_Y, 1)
+    collect(DIAG)
+    dots[...] = jnp.broadcast_to(dot[0], (tokens, tokens)).T[0:8, :]
+    for r in range(1, dp):
+        start(over_dp(dots, dotr.at[z], d_s.at[r], d_r.at[r], (z + r) % dp))
+    back_weights(DIAG, 1)
+    for i, (held, out_ref) in enumerate(((ggs, gg_ref), (gus, gu_ref))):
+        copy = pltpu.make_async_copy(held, out_ref, l_s.at[3 + i])
+        copy.start()
+        stores.append(copy)
+
+    for r in range(1, dp):
+        source = (z + dp - r) % dp
+        over_dp(
+            pr.at[pl.ds(0, per)], zr.at[source], z_s.at[r], z_r.at[r], source
+        ).wait_recv()
+    sums = []
+    for jj in range(per):
+        j = z * per + jj
+        total = pr[j].astype(jnp.float32)
+        for r in range(1, dp):
+            total = total + zr[(z + r) % dp, jj].astype(jnp.float32)
+        sums.append(total)
+        part = jnp.sum(total * un[j], axis=0, keepdims=True)
+        gsend[jj] = jnp.broadcast_to(part, (8, block))
+    for m in range(1, 8):
+        start(remote(gsend, gsum.at[b], e_s.at[m], e_r.at[m], m))
+    total_dot = dots[...]
+    for r in range(1, dp):
+        source = (z + dp - r) % dp
+        over_dp(dots, dotr.at[source], d_s.at[r], d_r.at[r], source).wait_recv()
+        total_dot = total_dot + dotr[source]
+    means = jnp.broadcast_to(total_dot[0:1, :] / model, (tokens, tokens)).T[:, 0:1]
+    root = rm[:, 0:1]
+    for jj in range(per):
+        j = z * per + jj
+        value = (sums[jj] * gs[j] - un[j] * means) / root
+        gi_ref[:, jj * block : (jj + 1) * block] = value.astype(jnp.bfloat16)
+    total_gain = gsend[...]
+    for m in range(1, 8):
+        remote(gsend, gsum.at[at(m)], e_s.at[m], e_r.at[m], m).wait_recv()
+        total_gain = total_gain + gsum[at(m)]
+    for jj in range(per):
+        ggain_ref[:, jj * block : (jj + 1) * block] = total_gain[jj, 0:1, :]
+
+    for copy in sends:
+        copy.wait_send()
+    for r in range(1, dp):
+        over_dp(pr.at[pl.ds(0, per)], zr.at[z], z_s.at[r], z_r.at[r], (z + r) % dp).wait_send()
+    for copy in stores:
+        copy.wait()
+
+
+def by_kernel(dp, inputs, gain, w_gate, w_up, upstream):
+    tokens, model = inputs.shape
+    block, hidden = w_gate.shape
+    per = 8 // dp
+    bf16, f32 = jnp.bfloat16, jnp.float32
+    vmem = pl.BlockSpec(memory_space=pltpu.VMEM)
+    hbm = pl.BlockSpec(memory_space=pl.ANY)
+
+    def dma(*shape):
+        return pltpu.SemaphoreType.DMA(shape)
+
+    by_chunk = []
+    for _, width in chunks_of(hidden):
+        by_chunk += [
+            pltpu.VMEM((tokens, width), bf16),
+            pltpu.VMEM((tokens, width), bf16),
+            pltpu.VMEM((4, 2, 2, tokens, width), bf16),
+            pltpu.VMEM((4, 2, tokens, width), bf16),
+            pltpu.VMEM((2, 3, tokens, width), bf16),
+            pltpu.VMEM((2, 3, tokens, width), bf16),
+            pltpu.VMEM((2, 8, tokens, width), bf16),
+        ]
+    hid, grad_gate, grad_up, grad_input, grad_gain = pl.pallas_call(
+        functools.partial(plane_kernel, dp),
+        out_shape=(
+            jax.ShapeDtypeStruct((hidden, tokens), bf16),
+            jax.ShapeDtypeStruct((block, hidden), f32),
+            jax.ShapeDtypeStruct((block, hidden), f32),
+            jax.ShapeDtypeStruct((tokens, per * block), bf16),
+            jax.ShapeDtypeStruct((1, per * block), f32),
+        ),
+        in_specs=[vmem, vmem, hbm, hbm, vmem],
+        out_specs=(hbm, hbm, hbm, vmem, vmem),
+        scratch_shapes=[
+            pltpu.VMEM((8, tokens, block), bf16),
+            pltpu.VMEM((8, tokens, block), f32),
+            pltpu.VMEM((8, 1, block), f32),
+            pltpu.VMEM((tokens, 128), f32),
+            pltpu.VMEM((8, tokens, block), bf16),
+            pltpu.VMEM((4, block, 2 * tokens), bf16),
+            pltpu.VMEM((block, hidden), bf16),
+            pltpu.VMEM((block, hidden), bf16),
+            pltpu.VMEM((block, hidden), f32),
+            pltpu.VMEM((block, hidden), f32),
+            pltpu.VMEM((hidden, tokens), bf16),
+            pltpu.VMEM((4, 2 * tokens, block), f32),
+            pltpu.VMEM((8, tokens, block), bf16),
+            pltpu.VMEM((8, tokens, block), bf16),
+            pltpu.VMEM((dp, per, tokens, block), bf16),
+            pltpu.VMEM((8, tokens), f32),
+            pltpu.VMEM((dp, 8, tokens), f32),
+            pltpu.VMEM((8, per, 8, block), f32),
+            pltpu.VMEM((per, 8, block), f32),
+            *by_chunk,
+            dma(8), dma(8), dma(2, 4, 2), dma(2, 4, 2), dma(2, 2, 3), dma(2, 2, 3),
+            dma(2, 2, 8), dma(2, 2, 8), dma(8), dma(8), dma(dp), dma(dp), dma(dp), dma(dp),
+            dma(8), dma(8), dma(5),
+        ],
+        compiler_params=pltpu.CompilerParams(
+            collective_id=0, has_side_effects=True, vmem_limit_bytes=60 * 2**20
+        ),
+        cost_estimate=pl.CostEstimate(
+            flops=48 * tokens * block * hidden * 2,
+            bytes_accessed=16 * block * hidden,
+            transcendentals=tokens * hidden,
+        ),
+    )(inputs, gain.reshape(1, model), w_gate, w_up, upstream.T)
+    return hid.T, grad_gate, grad_up, grad_input, grad_gain.reshape(per * block)
+
+
+def by_collectives(inputs, gain, w_gate, w_up, upstream):
     wide_input = inputs.astype(jnp.float32)
     root_mean = jnp.sqrt(jnp.mean(wide_input * wide_input, axis=1, keepdims=True) + 1e-05)
     unit_input = wide_input / root_mean
@@ -49,8 +535,10 @@
 
 
 def solution(mesh):
+    dp = mesh.shape["dp"]
+    by_chip = mesh.shape["blk"] == 8 and dp == 4
     return jax.shard_map(
-        per_device,
+        functools.partial(by_kernel, dp) if by_chip else by_collectives,
         mesh=mesh,
         in_specs=(P("blk", None), P(), P("blk", "dp"), P("blk", "dp"), P("blk", "dp")),
         out_specs=(P("blk", "dp"), P("blk", "dp"), P("blk", "dp"), P("blk", "dp"), P("dp")),

time: 283 us -> 120 us (0.42)
  waiting for transfers between devices: 168 us -> 0 us
  Pallas kernels: 0 us -> 109 us
  blocking collectives: 52.6 us -> 0 us
  matrix products: 25.2 us -> 0 us
  between operations: 13.9 us -> 0.64 us
  local copies, waits for them, and re-layouts: 16.9 us -> 8.5 us
  other arithmetic: 5.58 us -> 1.26 us
    pallas_call x0 -> x1, Pallas kernels: none -> 109 us  [by_kernel(): pl.pallas_call(functools.partial(plane_kernel, dp), out_shape=(jax.ShapeD...]
    unnamed x7 -> x0, waiting for transfers between devices: 88.9 us -> none
    all_gather x2 -> x0, waiting for transfers between devices: 66 us -> none  [the longest x1 34.1 us: per_device(): all_gate = lax.all_gather(back_gate, 'blk', axis=0, tiled=True)]
    all_to_all x2 -> x0, blocking collectives: 30.5 us -> none  [the longest x1 16.1 us: per_device(): lax.all_to_all(normed, 'blk', split_axis=1, concat_axis=0, tiled=True)]
    dot_general x6 -> x0, matrix products: 25.2 us -> none  [the longest x1 5.17 us: per_device(): jnp.dot(columns, w_up, preferred_element_type=jnp.float32)]
    psum x2 -> x0, blocking collectives: 22.1 us -> none  [the longest x1 12.4 us: per_device(): grad_gain = lax.psum(jnp.sum(own_sums * unit_slice, axis=0), 'blk')]
    reduce_scatter x1 -> x0, waiting for transfers between devices: 13.6 us -> none  [per_device(): lax.psum_scatter(part, 'dp', scatter_dimension=1, tiled=True)]
    unnamed x16 -> x8, local copies, waits for them, and re-layouts: 16.7 us -> 7.19 us
  transfers between devices with their start and end apart: 5 -> 0, of which waited for: 5 -> 0; matrix products, arithmetic and copies ran while one was open for 9% -> 0% of each run, Pallas kernels for 0% -> 0%
where the time goes in v3:
time: 120 us
  Pallas kernels  109 us (91%)
  local copies, waits for them, and re-layouts  8.5 us (7%)
  other arithmetic  1.26 us (1%)
    pallas_call x1, Pallas kernels, by_kernel(): pl.pallas_call(functools.partial(plane_kernel, dp), out_shape=(jax.ShapeD...  109 us
    unnamed x8, local copies, waits for them, and re-layouts  7.19 us

profile of v3, /device:TPU:0, one launch (start us, length us, event | category | flops | bytes accessed | tf_op | source)
XLA Modules:
  0.0 119.5 jit_solution(4335025904572874830)
XLA Ops:
  0.6 1.3 %reshape.16.gain_ref = f32[1,2560]{1,0:T(1,128)} reshape(f32[2560]{0:T(1024)} %param.6) | data formatting | bytes 20480 | tf_op jit(solution)/shard_map/reshape | solution.py:489
  1.9 109.1 %shard_map.92 = (bf16[1728,128]{1,0:T(8,128)(2,1)}, f32[320,1728]{1,0:T(8,128)}, f32[320,1728]{1,0:T(8,128)}, bf16[128,640]{1,0:T(8,128)(2,1)}, f32[1,640]{1,0:T(1,128)}) custom-call(bf16[128,2560]{1,0:T(8,128)(2,1)} %x_ref.1, f32[1,2560]{1,0:T(1,128)} %reshape.16.gain_ref, bf16[320,1728]{1,0:T(8,128)(2,1)} %wg_ref.1, bf16[320,1728]{1,0:T(8,128)(2,1)} %wu_ref.1, ...), custom_call_target="tpu_custom_call" | custom-call | flops 6794772480 | bytes 8847360 | tf_op jit(solution)/shard_map/pallas_call | solution.py:445
  111.1 1.3 %reduce = f32[640]{0:T(1024)} reduce(f32[1,640]{1,0:T(1,128)} %get-tuple-element.14, f32[]{:T(128)} %constant), dimensions={0}, to_apply=%get-tuple-element.14.reduce_sub_computation | reduce | bytes 5124 | tf_op jit(solution)/shard_map/pallas_call | solution.py:445
  112.3 1.8 %copy.14 = bf16[128,1728]{0,1:T(8,128)(2,1)} copy(bf16[128,1728]{0,1:T(8,128)(2,1)} %bitcast.2) | data formatting | bytes 884736
  114.1 0.0 copy-start
  114.1 3.3 %copy.15 = f32[320,1728]{1,0:T(8,128)} copy(f32[320,1728]{1,0:T(8,128)} %get-tuple-element.21) | data formatting | bytes 4423680
  117.5 0.0 copy-done
  117.5 0.0 copy-start.1
  117.5 1.4 %copy.16 = f32[320,1728]{1,0:T(8,128)} copy(f32[320,1728]{1,0:T(8,128)S(1)} %copy-done) | data formatting | bytes 4423680
  118.9 0.0 copy-done.1
  118.9 0.7 copy.17
Async XLA Ops:
  114.1 3.3 %copy-start = (f32[320,1728]{1,0:T(8,128)S(1)}, f32[320,1728]{1,0:T(8,128)}, u32[]{:S(2)}) copy-start(f32[320,1728]{1,0:T(8,128)} %get-tuple-element.22) | copy-start | bytes 6635524
  117.5 1.4 %copy-start.1 = (bf16[128,640]{1,0:T(8,128)(2,1)S(1)}, bf16[128,640]{1,0:T(8,128)(2,1)}, u32[]{:S(2)}) copy-start(bf16[128,640]{1,0:T(8,128)(2,1)} %get-tuple-element.23) | copy-start | bytes 491524

commit v4 on v3

--- a/solution.py
+++ b/solution.py
@@ -22,10 +22,10 @@
 def plane_kernel(
     dp, x_ref, gain_ref, wg_ref, wu_ref, up_ref,
     hid_ref, gg_ref, gu_ref, gi_ref, ggain_ref,
-    nb, un, gs, rm, xs, xt, wgs, wus, ggs, gus, hid, pacc, ps, pr, zr, dots, dotr, gsum, gsend,
+    gain_row, nb, un, gs, rm, xs, xt, wgs, wus, ggs, gus, hid, pacc, ps, pr, zr, dots, dotr, gsum, gsend, gtot, gz,
     ups0, hs0, pb0, rc0, sbuf0, rbuf0, full0,
     ups1, hs1, pb1, rc1, sbuf1, rbuf1, full1,
-    x_s, x_r, c_s, c_r, r_s, r_r, g_s, g_r, p_s, p_r, z_s, z_r, d_s, d_r, e_s, e_r, l_s,
+    x_s, x_r, c_s, c_r, r_s, r_r, g_s, g_r, p_s, p_r, z_s, z_r, d_s, d_r, e_s, e_r, f_s, f_r, l_s,
 ):
     b, z = lax.axis_index("blk"), lax.axis_index("dp")
     core, px, py = b % 2, (b // 2) % 2, b // 4
@@ -84,8 +84,11 @@
     ]
     for copy in loads:
         copy.start()
+    gain_load = pltpu.make_async_copy(gain_ref, gain_row.at[0], l_s.at[2])
+    gain_load.start()
+    gain_load.wait()
     for j in range(8):
-        gs[j] = gain_ref[:, j * block : (j + 1) * block]
+        gs[j] = gain_row[:, j * block : (j + 1) * block]
 
     def norm_rows(rows):
         wide = x_ref[rows, :].astype(jnp.float32)
@@ -107,9 +110,17 @@
         sends.append(copy)
         return copy
 
-    for mask in (6, 7, 2, 3, 4, 5, 1):
-        start(remote(nb.at[at(mask)], xs.at[b], x_s.at[mask], x_r.at[mask], mask))
+    def send_normed(mask):
+        copy = remote(nb.at[at(mask)], xs.at[b], x_s.at[mask], x_r.at[mask], mask)
+        copy.start()
+        return copy
+
+    far = [send_normed(mask) for mask in (6, 7)]
+    sends.append(send_normed(1))
     xs[b] = nb[b]
+    for copy in far:
+        copy.wait_send()
+    sends.extend(send_normed(mask) for mask in (2, 4, 3, 5))
     for copy in loads:
         copy.wait()
 
@@ -323,7 +334,7 @@
     back_inputs(ACROSS_Y, 0)
     forward_last(0)
     hid[chunks[1][0] : hidden, :] = hs[1][...].T
-    stores = [pltpu.make_async_copy(hid, hid_ref, l_s.at[2])]
+    stores = [pltpu.make_async_copy(hid, hid_ref, l_s.at[3])]
     stores[0].start()
     back_weights(ACROSS_X, 0)
     forward_first(1)
@@ -351,9 +362,9 @@
 
         for c in range(2):
             j = first + c
-            dot[0] = dot[0] + jnp.sum(
-                pr[j].astype(jnp.float32) * gs[j] * un[j], axis=1, keepdims=True
-            )
+            scaled = pr[j].astype(jnp.float32) * un[j]
+            dot[0] = dot[0] + jnp.sum(scaled * gs[j], axis=1, keepdims=True)
+            gsend[j] = jnp.sum(scaled, axis=0, keepdims=True)
 
     other_core(ACROSS_X, 1)
     back_inputs(ACROSS_X, 1)
@@ -369,14 +380,24 @@
     collect(ACROSS_Y)
     back_weights(ACROSS_Y, 1)
     collect(DIAG)
+    for m in range(1, 8):
+        start(remote(gsend, gsum.at[b], e_s.at[m], e_r.at[m], m))
     dots[...] = jnp.broadcast_to(dot[0], (tokens, tokens)).T[0:8, :]
     for r in range(1, dp):
         start(over_dp(dots, dotr.at[z], d_s.at[r], d_r.at[r], (z + r) % dp))
     back_weights(DIAG, 1)
     for i, (held, out_ref) in enumerate(((ggs, gg_ref), (gus, gu_ref))):
-        copy = pltpu.make_async_copy(held, out_ref, l_s.at[3 + i])
+        copy = pltpu.make_async_copy(held, out_ref, l_s.at[4 + i])
         copy.start()
         stores.append(copy)
+    total_gain = gsend[...]
+    for m in range(1, 8):
+        remote(gsend, gsum.at[at(m)], e_s.at[m], e_r.at[m], m).wait_recv()
+        total_gain = total_gain + gsum[at(m)]
+    gtot[...] = total_gain
+    for r in range(1, dp):
+        to = (z + r) % dp
+        start(over_dp(gtot.at[pl.ds(to * per, per)], gz.at[z], f_s.at[r], f_r.at[r], to))
 
     for r in range(1, dp):
         source = (z + dp - r) % dp
@@ -390,10 +411,6 @@
         for r in range(1, dp):
             total = total + zr[(z + r) % dp, jj].astype(jnp.float32)
         sums.append(total)
-        part = jnp.sum(total * un[j], axis=0, keepdims=True)
-        gsend[jj] = jnp.broadcast_to(part, (8, block))
-    for m in range(1, 8):
-        start(remote(gsend, gsum.at[b], e_s.at[m], e_r.at[m], m))
     total_dot = dots[...]
     for r in range(1, dp):
         source = (z + dp - r) % dp
@@ -405,18 +422,41 @@
         j = z * per + jj
         value = (sums[jj] * gs[j] - un[j] * means) / root
         gi_ref[:, jj * block : (jj + 1) * block] = value.astype(jnp.bfloat16)
-    total_gain = gsend[...]
-    for m in range(1, 8):
-        remote(gsend, gsum.at[at(m)], e_s.at[m], e_r.at[m], m).wait_recv()
-        total_gain = total_gain + gsum[at(m)]
+    total_gain = gtot[pl.ds(z * per, per)]
+    for r in range(1, dp):
+        source = (z + dp - r) % dp
+        over_dp(
+            gtot.at[pl.ds(0, per)], gz.at[source], f_s.at[r], f_r.at[r], source
+        ).wait_recv()
+        total_gain = total_gain + gz[source]
     for jj in range(per):
-        ggain_ref[:, jj * block : (jj + 1) * block] = total_gain[jj, 0:1, :]
+        ggain_ref[:, jj * block : (jj + 1) * block] = total_gain[jj]
 
     for copy in sends:
         copy.wait_send()
     for r in range(1, dp):
         over_dp(pr.at[pl.ds(0, per)], zr.at[z], z_s.at[r], z_r.at[r], (z + r) % dp).wait_send()
     for copy in stores:
+        copy.wait()
+
+
+PIECES = 4
+
+
+def copy_kernel(hid, gg, gu, gi, ggain, hid_ref, gg_ref, gu_ref, gi_ref, ggain_ref, sem):
+    rows = gg.shape[0] // PIECES
+    copies = []
+    for src, dst in ((gg, gg_ref), (gu, gu_ref)):
+        for i in range(PIECES):
+            part = pl.ds(i * rows, rows)
+            copies.append((src.at[part], dst.at[part]))
+    copies += [(hid, hid_ref), (gi, gi_ref), (ggain.at[0], ggain_ref)]
+    started = []
+    for i, (src, dst) in enumerate(copies):
+        copy = pltpu.make_async_copy(src, dst, sem.at[i])
+        copy.start()
+        started.append(copy)
+    for copy in started:
         copy.wait()
 
 
@@ -442,7 +482,7 @@
             pltpu.VMEM((2, 3, tokens, width), bf16),
             pltpu.VMEM((2, 8, tokens, width), bf16),
         ]
-    hid, grad_gate, grad_up, grad_input, grad_gain = pl.pallas_call(
+    results = pl.pallas_call(
         functools.partial(plane_kernel, dp),
         out_shape=(
             jax.ShapeDtypeStruct((hidden, tokens), bf16),
@@ -451,9 +491,10 @@
             jax.ShapeDtypeStruct((tokens, per * block), bf16),
             jax.ShapeDtypeStruct((1, per * block), f32),
         ),
-        in_specs=[vmem, vmem, hbm, hbm, vmem],
+        in_specs=[vmem, hbm, hbm, hbm, vmem],
         out_specs=(hbm, hbm, hbm, vmem, vmem),
         scratch_shapes=[
+            pltpu.VMEM((1, model), f32),
             pltpu.VMEM((8, tokens, block), bf16),
             pltpu.VMEM((8, tokens, block), f32),
             pltpu.VMEM((8, 1, block), f32),
@@ -471,12 +512,14 @@
             pltpu.VMEM((dp, per, tokens, block), bf16),
             pltpu.VMEM((8, tokens), f32),
             pltpu.VMEM((dp, 8, tokens), f32),
-            pltpu.VMEM((8, per, 8, block), f32),
-            pltpu.VMEM((per, 8, block), f32),
+            pltpu.VMEM((8, 8, 1, block), f32),
+            pltpu.VMEM((8, 1, block), f32),
+            pltpu.VMEM((8, 1, block), f32),
+            pltpu.VMEM((dp, per, 1, block), f32),
             *by_chunk,
             dma(8), dma(8), dma(2, 4, 2), dma(2, 4, 2), dma(2, 2, 3), dma(2, 2, 3),
             dma(2, 2, 8), dma(2, 2, 8), dma(8), dma(8), dma(dp), dma(dp), dma(dp), dma(dp),
-            dma(8), dma(8), dma(5),
+            dma(8), dma(8), dma(dp), dma(dp), dma(6),
         ],
         compiler_params=pltpu.CompilerParams(
             collective_id=0, has_side_effects=True, vmem_limit_bytes=60 * 2**20
@@ -486,8 +529,18 @@
             bytes_accessed=16 * block * hidden,
             transcendentals=tokens * hidden,
         ),
-    )(inputs, gain.reshape(1, model), w_gate, w_up, upstream.T)
-    return hid.T, grad_gate, grad_up, grad_input, grad_gain.reshape(per * block)
+    )(inputs, gain, w_gate, w_up, upstream.T)
+    shapes = [jax.ShapeDtypeStruct(a.shape, a.dtype) for a in results]
+    shapes[-1] = jax.ShapeDtypeStruct((per * block,), f32)
+    hid, grad_gate, grad_up, grad_input, grad_gain = pl.pallas_call(
+        copy_kernel,
+        out_shape=shapes,
+        in_specs=[hbm] * 5,
+        out_specs=[hbm] * 5,
+        scratch_shapes=[dma(2 * PIECES + 3)],
+        compiler_params=pltpu.CompilerParams(vmem_limit_bytes=60 * 2**20),
+    )(*results)
+    return hid.T, grad_gate, grad_up, grad_input, grad_gain
 
 
 def by_collectives(inputs, gain, w_gate, w_up, upstream):

time: 120 us -> 264 us (2.20); the launches traced: 120 us -> 260 us
  Pallas kernels: 109 us -> 259 us
  local copies, waits for them, and re-layouts: 8.5 us -> 0 us
    pallas_call x0 -> x1, Pallas kernels: none -> 159 us  [by_kernel(): pl.pallas_call(copy_kernel, out_shape=shapes, in_specs=[hbm] * 5, out_spe...]
    pallas_call x1, Pallas kernels: 109 us -> 100 us  [by_kernel(): pl.pallas_call(functools.partial(plane_kernel, dp), out_shape=(jax.ShapeD...]
    unnamed x8 -> x0, local copies, waits for them, and re-layouts: 7.19 us -> none
where the time goes in v4:
time: 264 us; the launch traced here: 260 us
  Pallas kernels  259 us (98%)
    pallas_call x1, Pallas kernels, by_kernel(): pl.pallas_call(copy_kernel, out_shape=shapes, in_specs=[hbm] * 5, out_spe...  159 us
    pallas_call x1, Pallas kernels, by_kernel(): pl.pallas_call(functools.partial(plane_kernel, dp), out_shape=(jax.ShapeD...  100 us

profile of v4, /device:TPU:0, one launch (start us, length us, event | category | flops | bytes accessed | tf_op | source)
XLA Modules:
  0.0 259.7 jit_solution(9178501389795970675)
XLA Ops:
  0.6 100.3 %shard_map.92 = (bf16[1728,128]{1,0:T(8,128)(2,1)}, f32[320,1728]{1,0:T(8,128)}, f32[320,1728]{1,0:T(8,128)}, bf16[128,640]{1,0:T(8,128)(2,1)}, f32[1,640]{1,0:T(1,128)}) custom-call(bf16[128,2560]{1,0:T(8,128)(2,1)} %x_ref.1, f32[2560]{0:T(1024)} %gain_ref.1, bf16[320,1728]{1,0:T(8,128)(2,1)} %wg_ref.1, bf16[320,1728]{1,0:T(8,128)(2,1)} %wu_ref.1, ...), custom_call_target="tpu_custom_call" | custom-call | flops 6794772480 | bytes 8847360 | tf_op jit(solution)/shard_map/pallas_call | solution.py:485
  100.9 158.6 %shard_map.93 = (bf16[1728,128]{1,0:T(8,128)(2,1)}, f32[320,1728]{1,0:T(8,128)}, f32[320,1728]{1,0:T(8,128)}, bf16[128,640]{1,0:T(8,128)(2,1)}, f32[640]{0:T(1024)}) custom-call(bf16[1728,128]{1,0:T(8,128)(2,1)} %get-tuple-element.15.hid, f32[320,1728]{1,0:T(8,128)} %get-tuple-element.16.gg, f32[320,1728]{1,0:T(8,128)} %get-tuple-element.17.gu, ...), custom_call_target="tpu_custom_call" | custom-call | tf_op jit(solution)/shard_map/pallas_call | solution.py:535

commit v5 on v4

--- a/solution.py
+++ b/solution.py
@@ -203,6 +203,8 @@
         pass_on(1, OWN, ACROSS_Y, h)
         pass_on(0, OWN, 1, h)
         pass_on(1, OWN, 1, h)
+
+    def second_sends(h):
         pass_on(1, OWN, ACROSS_X, h)
         pass_on(0, OWN, ACROSS_Y, h)
 
@@ -319,6 +321,7 @@
     for mask in (OWN, ACROSS_X, ACROSS_Y, DIAG):
         xt[SLOT[mask]] = columns(mask).T
     activate(0)
+    second_sends(0)
     send_sum(ACROSS_Y, 0, 2, ACROSS_Y, 1, extra=0)
     send_sum(ACROSS_X, 1, 2, ACROSS_X, 1, extra=0)
     hid[0 : chunks[0][1], :] = hs[0][...].T
@@ -326,6 +329,7 @@
     activate(1)
     other_core(OWN, 0)
     back_inputs(OWN, 0)
+    second_sends(1)
     back_weights(OWN, 0)
     forward_second(0)
     other_core(ACROSS_X, 0)
@@ -443,21 +447,30 @@
 PIECES = 4
 
 
-def copy_kernel(hid, gg, gu, gi, ggain, hid_ref, gg_ref, gu_ref, gi_ref, ggain_ref, sem):
+def copy_kernel(
+    hid, gg, gu, gi, ggain, hid_ref, gg_ref, gu_ref, gi_ref, ggain_ref,
+    hid_v, gg_v, gu_v, gi_v, ggain_v, in_sem, out_sem,
+):
     rows = gg.shape[0] // PIECES
-    copies = []
-    for src, dst in ((gg, gg_ref), (gu, gu_ref)):
-        for i in range(PIECES):
-            part = pl.ds(i * rows, rows)
-            copies.append((src.at[part], dst.at[part]))
-    copies += [(hid, hid_ref), (gi, gi_ref), (ggain.at[0], ggain_ref)]
-    started = []
-    for i, (src, dst) in enumerate(copies):
-        copy = pltpu.make_async_copy(src, dst, sem.at[i])
-        copy.start()
-        started.append(copy)
-    for copy in started:
-        copy.wait()
+    ways = []
+    for i in range(PIECES):
+        part = pl.ds(i * rows, rows)
+        for src, held, dst in ((gg, gg_v, gg_ref), (gu, gu_v, gu_ref)):
+            ways.append((src.at[part], held.at[part], held.at[part], dst.at[part]))
+    ways += [
+        (hid, hid_v, hid_v, hid_ref),
+        (gi, gi_v, gi_v, gi_ref),
+        (ggain, ggain_v, ggain_v.at[0], ggain_ref),
+    ]
+    loads = [pltpu.make_async_copy(w[0], w[1], in_sem.at[i]) for i, w in enumerate(ways)]
+    stores = [pltpu.make_async_copy(w[2], w[3], out_sem.at[i]) for i, w in enumerate(ways)]
+    for load in loads:
+        load.start()
+    for load, store in zip(loads, stores):
+        load.wait()
+        store.start()
+    for store in stores:
+        store.wait()
 
 
 def by_kernel(dp, inputs, gain, w_gate, w_up, upstream):
@@ -537,7 +550,11 @@
         out_shape=shapes,
         in_specs=[hbm] * 5,
         out_specs=[hbm] * 5,
-        scratch_shapes=[dma(2 * PIECES + 3)],
+        scratch_shapes=[
+            *(pltpu.VMEM(a.shape, a.dtype) for a in results),
+            dma(2 * PIECES + 3),
+            dma(2 * PIECES + 3),
+        ],
         compiler_params=pltpu.CompilerParams(vmem_limit_bytes=60 * 2**20),
     )(*results)
     return hid.T, grad_gate, grad_up, grad_input, grad_gain

time: 264 us -> 110 us (0.42)
  the two profiles are of different devices: /device:TPU:0 before, /device:TPU:5 now
where the time goes in v5:
time: 110 us
  Pallas kernels  109 us (99%)
    pallas_call x1, Pallas kernels, by_kernel(): pl.pallas_call(functools.partial(plane_kernel, dp), out_shape=(jax.ShapeD...  104 us
    pallas_call x1, Pallas kernels, by_kernel(): pl.pallas_call(copy_kernel, out_shape=shapes, in_specs=[hbm] * 5, out_spe...  4.5 us

profile of v5, /device:TPU:5, one launch (start us, length us, event | category | flops | bytes accessed | tf_op | source)
XLA Modules:
  0.0 109.5 jit_solution(8051231647618360450)
XLA Ops:
  0.6 104.2 %shard_map.92 = (bf16[1728,128]{1,0:T(8,128)(2,1)}, f32[320,1728]{1,0:T(8,128)}, f32[320,1728]{1,0:T(8,128)}, bf16[128,640]{1,0:T(8,128)(2,1)}, f32[1,640]{1,0:T(1,128)}) custom-call(bf16[128,2560]{1,0:T(8,128)(2,1)} %x_ref.1, f32[2560]{0:T(1024)} %gain_ref.1, bf16[320,1728]{1,0:T(8,128)(2,1)} %wg_ref.1, bf16[320,1728]{1,0:T(8,128)(2,1)} %wu_ref.1, ...), custom_call_target="tpu_custom_call" | custom-call | flops 6794772480 | bytes 8847360 | tf_op jit(solution)/shard_map/pallas_call | solution.py:498
  104.9 4.5 %shard_map.93 = (bf16[1728,128]{1,0:T(8,128)(2,1)}, f32[320,1728]{1,0:T(8,128)}, f32[320,1728]{1,0:T(8,128)}, bf16[128,640]{1,0:T(8,128)(2,1)}, f32[640]{0:T(1024)}) custom-call(bf16[1728,128]{1,0:T(8,128)(2,1)} %get-tuple-element.15.hid, f32[320,1728]{1,0:T(8,128)} %get-tuple-element.16.gg, f32[320,1728]{1,0:T(8,128)} %get-tuple-element.17.gu, ...), custom_call_target="tpu_custom_call" | custom-call | tf_op jit(solution)/shard_map/pallas_call | solution.py:548

commit v6 on v5

--- a/solution.py
+++ b/solution.py
@@ -20,9 +20,9 @@
 
 
 def plane_kernel(
-    dp, x_ref, gain_ref, wg_ref, wu_ref, up_ref,
+    dp, x_hbm, gain_ref, wg_ref, wu_ref, up_hbm,
     hid_ref, gg_ref, gu_ref, gi_ref, ggain_ref,
-    gain_row, nb, un, gs, rm, xs, xt, wgs, wus, ggs, gus, hid, pacc, ps, pr, zr, dots, dotr, gsum, gsend, gtot, gz,
+    x_ref, up_ref, gain_row, nb, un, gs, rm, xs, xt, wgs, wus, ggs, gus, hid, pacc, ps, pr, zr, dots, dotr, gsum, gsend, gtot, gz,
     ups0, hs0, pb0, rc0, sbuf0, rbuf0, full0,
     ups1, hs1, pb1, rc1, sbuf1, rbuf1, full1,
     x_s, x_r, c_s, c_r, r_s, r_r, g_s, g_r, p_s, p_r, z_s, z_r, d_s, d_r, e_s, e_r, f_s, f_r, l_s,
@@ -64,13 +64,21 @@
             device_id={"dp": to}, device_id_type=MESH,
         )
 
-    def row_loop(body):
+    def row_loop(body, rows=ROWS):
         def step(i, carry):
-            body(pl.ds(pl.multiple_of(i * ROWS, ROWS), ROWS))
+            body(pl.ds(pl.multiple_of(i * rows, rows), rows))
             return carry
 
-        lax.fori_loop(0, tokens // ROWS, step, 0)
-
+        lax.fori_loop(0, tokens // rows, step, 0)
+
+    loads = [
+        pltpu.make_async_copy(src, dst, l_s.at[i])
+        for i, (src, dst) in enumerate(
+            ((x_hbm, x_ref), (gain_ref, gain_row.at[0]), (wg_ref, wgs), (wu_ref, wus), (up_hbm, up_ref))
+        )
+    ]
+    for copy in loads:
+        copy.start()
     barrier = pltpu.get_barrier_semaphore()
     for mask in range(1, 8):
         pl.semaphore_signal(barrier, inc=1, device_id={"blk": at(mask)}, device_id_type=MESH)
@@ -78,29 +86,22 @@
         pl.semaphore_signal(
             barrier, inc=1, device_id={"dp": (z + r) % dp}, device_id_type=MESH
         )
-    loads = [
-        pltpu.make_async_copy(wg_ref, wgs, l_s.at[0]),
-        pltpu.make_async_copy(wu_ref, wus, l_s.at[1]),
-    ]
-    for copy in loads:
-        copy.start()
-    gain_load = pltpu.make_async_copy(gain_ref, gain_row.at[0], l_s.at[2])
-    gain_load.start()
-    gain_load.wait()
+    for copy in loads[:2]:
+        copy.wait()
     for j in range(8):
         gs[j] = gain_row[:, j * block : (j + 1) * block]
 
     def norm_rows(rows):
         wide = x_ref[rows, :].astype(jnp.float32)
         root = jnp.sqrt(jnp.mean(wide * wide, axis=1, keepdims=True) + 1e-05)
-        rm[rows, :] = jnp.broadcast_to(root, (ROWS, 128))
+        rm[rows, :] = jnp.broadcast_to(root, (2 * ROWS, 128))
         unit = wide / root
         for j in range(8):
             piece = unit[:, j * block : (j + 1) * block]
             un[j, rows, :] = piece
             nb[j, rows, :] = (piece * gs[j]).astype(jnp.bfloat16)
 
-    row_loop(norm_rows)
+    row_loop(norm_rows, 2 * ROWS)
     pl.semaphore_wait(barrier, 7 + dp - 1)
 
     sends = []
@@ -121,7 +122,7 @@
     for copy in far:
         copy.wait_send()
     sends.extend(send_normed(mask) for mask in (2, 4, 3, 5))
-    for copy in loads:
+    for copy in loads[2:]:
         copy.wait()
 
     def columns(mask):
@@ -338,7 +339,7 @@
     back_inputs(ACROSS_Y, 0)
     forward_last(0)
     hid[chunks[1][0] : hidden, :] = hs[1][...].T
-    stores = [pltpu.make_async_copy(hid, hid_ref, l_s.at[3])]
+    stores = [pltpu.make_async_copy(hid, hid_ref, l_s.at[5])]
     stores[0].start()
     back_weights(ACROSS_X, 0)
     forward_first(1)
@@ -391,7 +392,7 @@
         start(over_dp(dots, dotr.at[z], d_s.at[r], d_r.at[r], (z + r) % dp))
     back_weights(DIAG, 1)
     for i, (held, out_ref) in enumerate(((ggs, gg_ref), (gus, gu_ref))):
-        copy = pltpu.make_async_copy(held, out_ref, l_s.at[4 + i])
+        copy = pltpu.make_async_copy(held, out_ref, l_s.at[6 + i])
         copy.start()
         stores.append(copy)
     total_gain = gsend[...]
@@ -504,9 +505,11 @@
             jax.ShapeDtypeStruct((tokens, per * block), bf16),
             jax.ShapeDtypeStruct((1, per * block), f32),
         ),
-        in_specs=[vmem, hbm, hbm, hbm, vmem],
+        in_specs=[hbm] * 5,
         out_specs=(hbm, hbm, hbm, vmem, vmem),
         scratch_shapes=[
+            pltpu.VMEM((tokens, model), bf16),
+            pltpu.VMEM((hidden, tokens), bf16),
             pltpu.VMEM((1, model), f32),
             pltpu.VMEM((8, tokens, block), bf16),
             pltpu.VMEM((8, tokens, block), f32),
@@ -532,7 +535,7 @@
             *by_chunk,
             dma(8), dma(8), dma(2, 4, 2), dma(2, 4, 2), dma(2, 2, 3), dma(2, 2, 3),
             dma(2, 2, 8), dma(2, 2, 8), dma(8), dma(8), dma(dp), dma(dp), dma(dp), dma(dp),
-            dma(8), dma(8), dma(dp), dma(dp), dma(6),
+            dma(8), dma(8), dma(dp), dma(dp), dma(8),
         ],
         compiler_params=pltpu.CompilerParams(
             collective_id=0, has_side_effects=True, vmem_limit_bytes=60 * 2**20

time: 110 us -> 108 us (0.982)
  Pallas kernels: 109 us -> 107 us
    pallas_call x1, Pallas kernels: 104 us -> 102 us  [by_kernel(): pl.pallas_call(functools.partial(plane_kernel, dp), out_shape=(jax.ShapeD...]
where the time goes in v6:
time: 108 us; the launch traced here: 107 us
  Pallas kernels  107 us (99%)
    pallas_call x1, Pallas kernels, by_kernel(): pl.pallas_call(functools.partial(plane_kernel, dp), out_shape=(jax.ShapeD...  102 us
    pallas_call x1, Pallas kernels, by_kernel(): pl.pallas_call(copy_kernel, out_shape=shapes, in_specs=[hbm] * 5, out_spe...  4.5 us

profile of v6, /device:TPU:5, one launch (start us, length us, event | category | flops | bytes accessed | tf_op | source)
XLA Modules:
  0.0 107.4 jit_solution(17327257550935877890)
XLA Ops:
  0.6 102.1 %shard_map.92 = (bf16[1728,128]{1,0:T(8,128)(2,1)}, f32[320,1728]{1,0:T(8,128)}, f32[320,1728]{1,0:T(8,128)}, bf16[128,640]{1,0:T(8,128)(2,1)}, f32[1,640]{1,0:T(1,128)}) custom-call(bf16[128,2560]{1,0:T(8,128)(2,1)} %x_hbm.1, f32[2560]{0:T(1024)} %gain_ref.1, bf16[320,1728]{1,0:T(8,128)(2,1)} %wg_ref.1, bf16[320,1728]{1,0:T(8,128)(2,1)} %wu_ref.1, ...), custom_call_target="tpu_custom_call" | custom-call | flops 6794772480 | bytes 8847360 | tf_op jit(solution)/shard_map/pallas_call | solution.py:499
  102.8 4.5 %shard_map.93 = (bf16[1728,128]{1,0:T(8,128)(2,1)}, f32[320,1728]{1,0:T(8,128)}, f32[320,1728]{1,0:T(8,128)}, bf16[128,640]{1,0:T(8,128)(2,1)}, f32[640]{0:T(1024)}) custom-call(bf16[1728,128]{1,0:T(8,128)(2,1)} %get-tuple-element.15.hid, f32[320,1728]{1,0:T(8,128)} %get-tuple-element.16.gg, f32[320,1728]{1,0:T(8,128)} %get-tuple-element.17.gu, ...), custom_call_target="tpu_custom_call" | custom-call | tf_op jit(solution)/shard_map/pallas_call | solution.py:551
